TPU v7x, 32 devices: a whole 2x2x4 slice. The times are simulated.
32 devices in a mesh: dp: 8 (over z, x), mp: 4 (over y, core).
Axes of the slice: x: 2, y: 2, z: 4, core: 2. Of those that a mesh axis runs over, the one named last changes fastest.
Arguments:
- tokens: bfloat16 [6144, 1472], P(('dp', 'mp')), may hold values from -6 to 6
- cotangent: bfloat16 [6144, 1472], P(('dp', 'mp')), may hold values from -9 to 9
- lengths: int32 [8, 2], P('dp'), may hold values from 1 to 672, as said below
- heads_in: float32 [3, 1472, 384], P(None, 'dp'), may hold values from -0.0546875 to 0.0546875
- heads_out: float32 [384, 1472], P(None, 'dp'), may hold values from -6 to 6
- expand_in: float32 [2, 1472, 3584], P(None, 'dp', 'mp'), may hold values from -0.15625 to 0.15625
- expand_out: float32 [3584, 1472], P('mp', 'dp'), may hold values from -0.09375 to 0.09375
- norm_gains: float32 [2, 1472], P(None, 'dp'), may hold values from 0.4 to 3.2
- bias_table: float32 [32, 6], replicated, may hold values from -4 to 4
- heads_in_first: float32 [3, 1472, 384], P(None, 'dp'), may hold values from -160 to 160
- heads_out_first: float32 [384, 1472], P(None, 'dp'), may hold values from -2.5 to 2.5
- expand_in_first: float32 [2, 1472, 3584], P(None, 'dp', 'mp'), may hold values from -28 to 28
- expand_out_first: float32 [3584, 1472], P('mp', 'dp'), may hold values from -40 to 40
- gains_first: float32 [2, 1472], P(None, 'dp'), may hold values from -56 to 56
- table_first: float32 [32, 6], replicated, may hold values from -40 to 40
- heads_in_second: float32 [3, 1472, 384], P(None, 'dp'), may hold values from 55.296 to 221.184
- heads_out_second: float32 [384, 1472], P(None, 'dp'), may hold values from 0.01536 to 0.06144
- expand_in_second: float32 [2, 1472, 3584], P(None, 'dp', 'mp'), may hold values from 1.536 to 6.144
- expand_out_second: float32 [3584, 1472], P('mp', 'dp'), may hold values from 3.93216 to 15.9744
- gains_second: float32 [2, 1472], P(None, 'dp'), may hold values from 6.144 to 24.576
- table_second: float32 [32, 6], replicated, may hold values from 4.2467327 to 16.98693
Outputs:
- layer_out: bfloat16 [6144, 1472], P(('dp', 'mp'))
- tokens_grad: float32 [6144, 1472], P(('dp', 'mp'))
- heads_in_moment: float32 [3, 1472, 384], P(None, 'dp')
- heads_in_square: float32 [3, 1472, 384], P(None, 'dp')
- heads_in_new: float32 [3, 1472, 384], P(None, 'dp')
- heads_in_copy: bfloat16 [3, 1472, 384], P(None, 'dp')
- heads_out_moment: float32 [384, 1472], P(None, 'dp')
- heads_out_square: float32 [384, 1472], P(None, 'dp')
- heads_out_new: float32 [384, 1472], P(None, 'dp')
- heads_out_copy: bfloat16 [384, 1472], P(None, 'dp')
- expand_in_moment: float32 [2, 1472, 3584], P(None, 'dp', 'mp')
- expand_in_square: float32 [2, 1472, 3584], P(None, 'dp', 'mp')
- expand_in_new: float32 [2, 1472, 3584], P(None, 'dp', 'mp')
- expand_in_copy: bfloat16 [2, 1472, 3584], P(None, 'dp', 'mp')
- expand_out_moment: float32 [3584, 1472], P('mp', 'dp')
- expand_out_square: float32 [3584, 1472], P('mp', 'dp')
- expand_out_new: float32 [3584, 1472], P('mp', 'dp')
- expand_out_copy: bfloat16 [3584, 1472], P('mp', 'dp')
- gains_moment: float32 [2, 1472], P(None, 'dp')
- gains_square: float32 [2, 1472], P(None, 'dp')
- gains_new: float32 [2, 1472], P(None, 'dp')
- gains_copy: bfloat16 [2, 1472], P(None, 'dp')
- table_moment: float32 [32, 6], replicated
- table_square: float32 [32, 6], replicated
- table_new: float32 [32, 6], replicated
- table_copy: bfloat16 [32, 6], replicated
- weight_norms: float32 [2, 10], replicated
Inputs may be any that keep to these rules, and one draw needn't show every extreme that they name: Group g's two items fill positions 0 to lengths[g, 0] + lengths[g, 1] - 1 of the group, the rest being padding; the sum is at most 768. Each group's longer item has more than 576 positions, and some group's has exactly 672.
All inputs are finite; a program needn't handle non-finite values.
Results may differ from a plain program's by a relative error of at most 0.024.
The roundings to bfloat16 on the way count: a program that leaves them out, or rounds other values in their place, can miss the bound.
Values may be sent and summed in bfloat16 or wider, within the bound.
A program may use at most 192 MiB of HBM per device.

v0:
```python
from functools import partial

import jax
import jax.numpy as jnp
from jax import lax
from jax.sharding import PartitionSpec as P

HEADS = 6
HEAD_DIM = 64
STEP = 10
INNER = 384


norm_eps = 1e-06
beta_first = 0.9
beta_second = 0.999
adam_eps = 1e-06
weight_decay = 0.01
learn_rate = 0.4
masked_fill = -1000000000.0
bucket_edges = (12, 16, 23, 32, 46, 64, 91)
highest = lax.Precision.HIGHEST


def bucket_ids(offsets):
    distance = jnp.abs(offsets)
    coarse = jnp.full_like(distance, 8)
    for edge_value in bucket_edges:
        coarse = coarse + (distance >= edge_value).astype(jnp.int32)
    nearby = jnp.where(distance < 8, distance, coarse)
    return nearby + 16 * (offsets > 0).astype(jnp.int32)


def rms_scale(hidden_rows, gain_vector):
    return (
        hidden_rows
        * lax.rsqrt(jnp.mean(hidden_rows * hidden_rows, axis=-1, keepdims=True) + norm_eps)
        * gain_vector
    )


def segment_of(positions, item_lengths):
    first_end = item_lengths[0]
    second_end = item_lengths[0] + item_lengths[1]
    return (positions >= first_end).astype(jnp.int32) + (positions >= second_end).astype(jnp.int32)


def offset_table(table_values, first_row, query_count, key_count):
    span_len = key_count + query_count - 1
    offsets = jnp.arange(span_len, dtype=jnp.int32) - (query_count - 1) - first_row
    bucket_range = jnp.arange(table_values.shape[0], dtype=jnp.int32)
    onehot = (bucket_ids(offsets)[:, None] == bucket_range[None, :]).astype(jnp.float32)
    return jnp.dot(onehot, table_values, precision=highest).T


def spread_rows(per_offset, query_count, key_count):
    head_count, span_len = per_offset.shape
    padded = jnp.concatenate([per_offset, jnp.zeros((head_count, 1), per_offset.dtype)], axis=1)
    tiled_rows = jnp.broadcast_to(padded[:, None, :], (head_count, query_count, span_len + 1))
    tiled_rows = tiled_rows.reshape(head_count, query_count * (span_len + 1))[
        :, : query_count * span_len
    ]
    skewed = tiled_rows.reshape(head_count, query_count, span_len)
    return skewed[:, :, query_count - 1 : query_count - 1 + key_count]


def contract_rows(left_side, right_side):
    return lax.dot_general(
        left_side, right_side, (((0,), (0,)), ((), ())), preferred_element_type=jnp.float32
    )


def contract_cols(left_side, right_side):
    return lax.dot_general(
        left_side, right_side, (((1,), (1,)), ((), ())), preferred_element_type=jnp.float32
    )


def lamb_parts(weight, gradient, first_moment, second, decay_rate):
    new_first = beta_first * first_moment + (1.0 - beta_first) * gradient
    new_second = beta_second * second + (1.0 - beta_second) * gradient * gradient
    first_fix = 1.0 - beta_first**STEP
    second_fix = 1.0 - beta_second**STEP
    step_dir = (
        new_first / first_fix / (jnp.sqrt(new_second / second_fix) + adam_eps) + decay_rate * weight
    )
    return (new_first, new_second, step_dir)


def sub_squares(values, sub_count):
    flat_values = values.reshape(sub_count, -1)
    return jnp.sum(flat_values * flat_values, axis=1)


def shards(
    tokens,
    cotangent,
    lengths,
    heads_in,
    heads_out,
    expand_in,
    expand_out,
    norm_gains,
    bias_table,
    heads_in_first,
    heads_out_first,
    expand_in_first,
    expand_out_first,
    gains_first,
    table_first,
    heads_in_second,
    heads_out_second,
    expand_in_second,
    expand_out_second,
    gains_second,
    table_second,
):
    local_rows = tokens.shape[0]
    group_rows = local_rows * lax.axis_size("mp")
    first_row = lax.axis_index("mp") * local_rows
    shard_width = norm_gains.shape[1]
    full_in, full_out, full_expand, full_back, full_gains = (
        lax.all_gather(heads_in.astype(jnp.bfloat16), "dp", axis=1, tiled=True),
        lax.all_gather(heads_out.astype(jnp.bfloat16), "dp", axis=1, tiled=True),
        lax.all_gather(expand_in.astype(jnp.bfloat16), "dp", axis=1, tiled=True),
        lax.all_gather(expand_out.astype(jnp.bfloat16), "dp", axis=1, tiled=True),
        lax.all_gather(norm_gains.astype(jnp.bfloat16), "dp", axis=1, tiled=True),
    )
    gain_one = full_gains[0].astype(jnp.float32)
    gain_two = full_gains[1].astype(jnp.float32)
    inputs = tokens.astype(jnp.float32)
    normed, norm_one_pull = jax.vjp(rms_scale, inputs, gain_one)
    normed_low = normed.astype(jnp.bfloat16)
    queries = jnp.dot(normed_low, full_in[0], preferred_element_type=jnp.float32).astype(
        jnp.bfloat16
    )
    keys_own = jnp.dot(normed_low, full_in[1], preferred_element_type=jnp.float32).astype(
        jnp.bfloat16
    )
    values_own = jnp.dot(normed_low, full_in[2], preferred_element_type=jnp.float32).astype(
        jnp.bfloat16
    )
    keys_all, values_all = (
        lax.all_gather(keys_own, "mp", axis=0, tiled=True),
        lax.all_gather(values_own, "mp", axis=0, tiled=True),
    )
    query_heads = queries.reshape(local_rows, HEADS, HEAD_DIM)
    key_heads = keys_all.reshape(group_rows, HEADS, HEAD_DIM)
    value_heads = values_all.reshape(group_rows, HEADS, HEAD_DIM)
    item_lengths = lengths[0]
    query_pos = first_row + jnp.arange(local_rows, dtype=jnp.int32)
    key_pos = jnp.arange(group_rows, dtype=jnp.int32)
    allowed = (
        segment_of(query_pos, item_lengths)[:, None] == segment_of(key_pos, item_lengths)[None, :]
    )[None]

    def bias_of(table_values):
        return spread_rows(
            offset_table(table_values, first_row, local_rows, group_rows), local_rows, group_rows
        )

    position_bias, bias_pull = jax.vjp(bias_of, bias_table)

    def score_block():
        raw_scores = jnp.einsum(
            "qhd,khd->hqk", query_heads, key_heads, preferred_element_type=jnp.float32
        )
        return jnp.where(allowed, raw_scores + position_bias, masked_fill)

    scores = score_block()
    row_max = jnp.max(scores, axis=-1, keepdims=True)
    exp_scores = jnp.exp(scores - row_max)
    row_total = jnp.sum(exp_scores, axis=-1, keepdims=True)
    log_total = row_max + jnp.log(row_total)
    soft_low = (exp_scores / row_total).astype(jnp.bfloat16)
    mixed_heads = jnp.einsum(
        "hqk,khd->qhd", soft_low, value_heads, preferred_element_type=jnp.float32
    )
    mixed_low = mixed_heads.reshape(local_rows, INNER).astype(jnp.bfloat16)
    attended = jnp.dot(mixed_low, full_out, preferred_element_type=jnp.float32)
    residual_one = inputs + attended
    normed_two, norm_two_pull = jax.vjp(rms_scale, residual_one, gain_two)
    normed_all = lax.all_gather(normed_two.astype(jnp.bfloat16), "mp", axis=0, tiled=True)
    gate_pre = jnp.dot(normed_all, full_expand[0], preferred_element_type=jnp.float32)
    up_pre = jnp.dot(normed_all, full_expand[1], preferred_element_type=jnp.float32)
    gelu_gate, gelu_pull = jax.vjp(partial(jax.nn.gelu, approximate=True), gate_pre)
    hidden_units = (gelu_gate * up_pre).astype(jnp.bfloat16)
    hidden_part = lax.slice_in_dim(hidden_units, 0, local_rows * lax.axis_size("mp"), axis=0)
    feed_out = lax.psum_scatter(
        jnp.dot(hidden_part, full_back, preferred_element_type=jnp.float32).astype(jnp.bfloat16),
        "mp",
        scatter_dimension=0,
        tiled=True,
    ).astype(jnp.float32)
    layer_out = (residual_one + feed_out).astype(jnp.bfloat16)
    key_used = (key_pos < item_lengths[0] + item_lengths[1]).astype(jnp.float32)
    row_used = lax.dynamic_slice_in_dim(key_used, first_row, local_rows, 0)
    upstream = cotangent.astype(jnp.float32) * row_used[:, None]
    upstream_all = lax.all_gather(upstream.astype(jnp.bfloat16), "mp", axis=0, tiled=True)
    hidden_grad = contract_cols(upstream_all, full_back)
    grad_expand_out = contract_rows(hidden_units, upstream_all)
    up_grad = (hidden_grad * gelu_gate).astype(jnp.bfloat16)
    gate_grad = gelu_pull(hidden_grad * up_pre)[0].astype(jnp.bfloat16)
    grad_expand_in = jnp.stack(
        [contract_rows(normed_all, gate_grad), contract_rows(normed_all, up_grad)]
    )
    up_rows = lax.slice_in_dim(up_grad, 0, local_rows * lax.axis_size("mp"), axis=0)
    normed_two_grad = lax.psum_scatter(
        contract_cols(gate_grad, full_expand[0]) + contract_cols(up_rows, full_expand[1]),
        "mp",
        scatter_dimension=0,
        tiled=True,
    )
    resid_norm_grad, gain_two_grad = norm_two_pull(normed_two_grad)
    residual_grad = upstream + resid_norm_grad
    attended_grad = residual_grad.astype(jnp.bfloat16)
    grad_heads_out = contract_rows(mixed_low, attended_grad)
    mixed_grad = (
        contract_cols(attended_grad, full_out)
        .astype(jnp.bfloat16)
        .reshape(local_rows, HEADS, HEAD_DIM)
    )
    scores = score_block()
    soft_full = jnp.exp(scores - log_total)
    soft_again = soft_full.astype(jnp.bfloat16)
    soft_grad = jnp.einsum(
        "qhd,khd->hqk", mixed_grad, value_heads, preferred_element_type=jnp.float32
    )
    row_corr = jnp.sum(soft_full * soft_grad, axis=-1, keepdims=True)
    scores_grad = (soft_full * (soft_grad - row_corr)).astype(jnp.bfloat16)
    query_grad = jnp.einsum(
        "hqk,khd->qhd", scores_grad, key_heads, preferred_element_type=jnp.float32
    )
    query_grad = query_grad.reshape(local_rows, INNER).astype(jnp.bfloat16)
    part_keys = jnp.einsum(
        "hqk,qhd->khd", scores_grad, query_heads, preferred_element_type=jnp.float32
    )
    part_values = jnp.einsum(
        "hqk,qhd->khd", soft_again, mixed_grad, preferred_element_type=jnp.float32
    )
    grad_table = bias_pull(scores_grad.astype(jnp.float32))[0]
    key_grad, value_grad = (
        lax.psum_scatter(
            part_keys.reshape(group_rows, INNER).astype(jnp.bfloat16),
            "mp",
            scatter_dimension=0,
            tiled=True,
        ).astype(jnp.float32),
        lax.psum_scatter(
            part_values.reshape(group_rows, INNER).astype(jnp.bfloat16),
            "mp",
            scatter_dimension=0,
            tiled=True,
        ).astype(jnp.float32),
    )
    key_low = key_grad.astype(jnp.bfloat16)
    value_low = value_grad.astype(jnp.bfloat16)
    grad_heads_in = jnp.stack(
        [
            contract_rows(normed_low, query_grad),
            contract_rows(normed_low, key_low),
            contract_rows(normed_low, value_low),
        ]
    )
    normed_grad = (
        contract_cols(query_grad, full_in[0])
        + contract_cols(key_low, full_in[1])
        + contract_cols(value_low, full_in[2])
    )
    input_norm_grad, gain_one_grad = norm_one_pull(normed_grad)
    tokens_grad = residual_grad + input_norm_grad
    gains_total, table_grad = lax.psum(
        (jnp.stack([gain_one_grad, gain_two_grad]), grad_table), ("dp", "mp")
    )
    gains_grad = lax.dynamic_slice_in_dim(
        gains_total, lax.axis_index("dp") * shard_width, shard_width, 1
    )
    head_in_part, head_out_part, expand_in_grad, expand_out_grad = (
        lax.psum_scatter(grad_heads_in, "dp", scatter_dimension=1, tiled=True),
        lax.psum_scatter(grad_heads_out, "dp", scatter_dimension=1, tiled=True),
        lax.psum_scatter(grad_expand_in, "dp", scatter_dimension=1, tiled=True),
        lax.psum_scatter(grad_expand_out, "dp", scatter_dimension=1, tiled=True),
    )
    head_in_grad, head_out_grad = (
        lax.psum(head_in_part.astype(jnp.bfloat16), "mp").astype(jnp.float32),
        lax.psum(head_out_part.astype(jnp.bfloat16), "mp").astype(jnp.float32),
    )
    weight_list = (heads_in, heads_out, expand_in, expand_out, norm_gains, bias_table)
    grad_list = (
        head_in_grad,
        head_out_grad,
        expand_in_grad,
        expand_out_grad,
        gains_grad,
        table_grad,
    )
    first_list = (
        heads_in_first,
        heads_out_first,
        expand_in_first,
        expand_out_first,
        gains_first,
        table_first,
    )
    second_list = (
        heads_in_second,
        heads_out_second,
        expand_in_second,
        expand_out_second,
        gains_second,
        table_second,
    )
    decay_list = (weight_decay, weight_decay, weight_decay, weight_decay, 0.0, 0.0)
    sub_list = (3, 1, 2, 1, 2, 1)
    results = [
        lamb_parts(
            weight_list[number],
            grad_list[number],
            first_list[number],
            second_list[number],
            decay_list[number],
        )
        for number in range(6)
    ]
    weight_sq = [sub_squares(weight_list[number], sub_list[number]) for number in range(6)]
    step_sq = [sub_squares(results[number][2], sub_list[number]) for number in range(6)]
    shared_scale = 1.0 / lax.axis_size("mp")
    weight_sums, step_sums = lax.psum(
        (
            jnp.concatenate(
                [
                    weight_sq[0] * shared_scale,
                    weight_sq[1] * shared_scale,
                    weight_sq[2],
                    weight_sq[3],
                    weight_sq[4] * shared_scale,
                ]
            ),
            jnp.concatenate(
                [
                    step_sq[0] * shared_scale,
                    step_sq[1] * shared_scale,
                    step_sq[2],
                    step_sq[3],
                    step_sq[4] * shared_scale,
                ]
            ),
        ),
        ("dp", "mp"),
    )
    weight_norm = jnp.sqrt(jnp.concatenate([weight_sums, weight_sq[5]]))
    step_norm = jnp.sqrt(jnp.concatenate([step_sums, step_sq[5]]))
    ratios = weight_norm / step_norm
    starts = (0, 3, 4, 6, 7, 9)
    outputs = [layer_out, tokens_grad]
    for number in range(6):
        weight = weight_list[number]
        sub_count = sub_list[number]
        ratio_part = ratios[starts[number] : starts[number] + sub_count]
        flat_weight = weight.reshape(sub_count, -1)
        flat_step = results[number][2].reshape(sub_count, -1)
        new_weight = (flat_weight - learn_rate * ratio_part[:, None] * flat_step).reshape(
            weight.shape
        )
        outputs = outputs + [
            results[number][0],
            results[number][1],
            new_weight,
            new_weight.astype(jnp.bfloat16),
        ]
    outputs = outputs + [jnp.stack([weight_norm, step_norm])]
    return tuple(outputs)


def solution(mesh):
    return jax.shard_map(
        shards,
        mesh=mesh,
        in_specs=(
            P(("dp", "mp"), None),
            P(("dp", "mp"), None),
            P("dp", None),
            P(None, "dp", None),
            P(None, "dp"),
            P(None, "dp", "mp"),
            P("mp", "dp"),
            P(None, "dp"),
            P(),
            P(None, "dp", None),
            P(None, "dp"),
            P(None, "dp", "mp"),
            P("mp", "dp"),
            P(None, "dp"),
            P(),
            P(None, "dp", None),
            P(None, "dp"),
            P(None, "dp", "mp"),
            P("mp", "dp"),
            P(None, "dp"),
            P(),
        ),
        out_specs=(
            P(("dp", "mp"), None),
            P(("dp", "mp"), None),
            P(None, "dp", None),
            P(None, "dp", None),
            P(None, "dp", None),
            P(None, "dp", None),
            P(None, "dp"),
            P(None, "dp"),
            P(None, "dp"),
            P(None, "dp"),
            P(None, "dp", "mp"),
            P(None, "dp", "mp"),
            P(None, "dp", "mp"),
            P(None, "dp", "mp"),
            P("mp", "dp"),
            P("mp", "dp"),
            P("mp", "dp"),
            P("mp", "dp"),
            P(None, "dp"),
            P(None, "dp"),
            P(None, "dp"),
            P(None, "dp"),
            P(),
            P(),
            P(),
            P(),
            P(),
        ),
        check_vma=False,
    )
```

profile of v0, /device:TPU:0, one launch (start us, length us, event | category | flops | bytes accessed | tf_op | source)
XLA Modules:
  0.0 1074.9 jit_solution(4372063738051846890)
XLA Ops:
  11.2 22.3 %all-gather = bf16[8,184,2]{1,2,0:T(2,128)(2,1)S(1)} all-gather(bf16[1,184,2]{1,2,0:T(2,128)(2,1)S(1)} %convert_bitcast_fusion), channel_id=1, replica_groups=mesh['dp'=8,'mp'=4] {'dp'}, dimensions={0}, use_global_device_ids=true | all-gather | bytes 6624 | tf_op jit(solution)/shard_map/all_gather | solution.py:127
  37.0 7.4 reshape.394
  48.9 8.5 reshape.395
  61.7 15.3 %all-gather.8.cloned.1.call-done = bf16[3,1472,384]{2,1,0:T(8,128)(2,1)} async-done(((bf16[3,184,384]{2,1,0:T(8,128)(2,1)}), bf16[3,1472,384]{2,1,0:T(8,128)(2,1)}) %all-gather.8.cloned.1.call-update) | async-done | bytes 3391504 | tf_op jit(solution)/shard_map/all_gather | solution.py:123
  81.3 7.5 all_gather.29
  91.7 7.9 all_gather.30
  108.0 11.0 %all-gather.10.cloned.1.call-done = bf16[384,1472]{0,1:T(8,128)(2,1)} async-done(((bf16[384,184]{0,1:T(8,128)(2,1)}), bf16[384,1472]{0,1:T(8,128)(2,1)}) %all-gather.10.cloned.1.call-update) | async-done | bytes 1130512 | tf_op jit(solution)/shard_map/all_gather | solution.py:124
  128.0 79.3 %all-gather.14.cloned.1.call-done = bf16[2,1472,896]{2,1,0:T(8,128)(2,1)} async-done(((bf16[2,184,896]{2,1,0:T(8,128)(2,1)}), bf16[2,1472,896]{2,1,0:T(8,128)(2,1)}) %all-gather.14.cloned.1.call-update) | async-done | bytes 5275664 | tf_op jit(solution)/shard_map/all_gather | solution.py:125
  207.4 24.3 %all-gather.12.cloned.1.call-done = bf16[768,1472]{1,0:T(8,128)(2,1)} async-done(((bf16[192,1472]{1,0:T(8,128)(2,1)}), bf16[768,1472]{1,0:T(8,128)(2,1)}) %all-gather.12.cloned.1.call-update) | async-done | bytes 2261008 | tf_op jit(solution)/shard_map/all_gather | solution.py:183
  231.6 6.8 fusion.12
  242.5 15.2 %all-gather.18.cloned.1.call-done = bf16[768,1472]{1,0:T(8,128)(2,1)} async-done(((bf16[192,1472]{1,0:T(8,128)(2,1)}), bf16[768,1472]{1,0:T(8,128)(2,1)}) %all-gather.18.cloned.1.call-update) | async-done | bytes 2261008 | tf_op jit(solution)/shard_map/all_gather | solution.py:199
  257.7 57.5 %all-gather.16.cloned.1.call-done = bf16[896,1472]{0,1:T(8,128)(2,1)} async-done(((bf16[896,184]{0,1:T(8,128)(2,1)}), bf16[896,1472]{0,1:T(8,128)(2,1)}) %all-gather.16.cloned.1.call-update) | async-done | bytes 2637840 | tf_op jit(solution)/shard_map/all_gather | solution.py:126
  315.2 9.5 multiply_convert_fusion.1
  342.6 11.7 %reduce-scatter.27.cloned.1.call-start = ((), (), s32[]{:S(2)}) async-start(), calls=%async_computation.19 | async-start | bytes 737280
  355.7 27.2 %reduce-scatter.19.cloned.1.call-done = f32[192,1472]{1,0:T(8,128)} async-done(((f32[768,1472]{1,0:T(8,128)}), f32[192,1472]{1,0:T(8,128)}) %reduce-scatter.19.cloned.1.call-update) | async-done | bytes 1130512 | tf_op jit(solution)/shard_map/reduce_scatter | solution.py:208
  385.9 32.7 %reduce-scatter.17.cloned.1.call-done = bf16[192,1472]{1,0:T(8,128)(2,1)} async-done(((bf16[768,1472]{1,0:T(8,128)(2,1)}), bf16[192,1472]{1,0:T(8,128)(2,1)}) %reduce-scatter.17.cloned.1.call-update) | async-done | bytes 565264 | tf_op jit(solution)/shard_map/reduce_scatter | solution.py:189
  455.8 22.0 %reduce-scatter.25.cloned.1.call-done = bf16[192,384]{1,0:T(8,128)(2,1)} async-done(((bf16[768,384]{1,0:T(8,128)(2,1)}), bf16[192,384]{1,0:T(8,128)(2,1)}) %reduce-scatter.25.cloned.1.call-update) | async-done | bytes 147472
  517.0 7.0 reshape.405
  534.6 41.3 %psum.45 = f32[2,1472]{1,0:T(2,128)S(1)} all-reduce(f32[2,1472]{1,0:T(2,128)S(1)} %pad_maximum_fusion.2), channel_id=1, replica_groups=mesh['dp'=8,'mp'=4] {'dp','mp'}, use_global_device_ids=true, to_apply=%region_30.31 | all-reduce | flops 2944 | bytes 23552 | tf_op jit(solution)/shard_map/psum | solution.py:272
  588.4 68.3 %reduce-scatter.29.cloned.1.call-done = f32[384,184]{0,1:T(8,128)} async-done(((f32[384,1472]{0,1:T(8,128)}), f32[384,184]{0,1:T(8,128)}) %reduce-scatter.29.cloned.1.call-update) | async-done | bytes 282640
  658.3 126.6 %reduce-scatter.21.cloned.1.call-done = f32[3,184,384]{2,1,0:T(8,128)} async-done(((f32[3,1472,384]{2,1,0:T(8,128)}), f32[3,184,384]{2,1,0:T(8,128)}) %reduce-scatter.21.cloned.1.call-update) | async-done | bytes 847888 | tf_op jit(solution)/shard_map/reduce_scatter | solution.py:279
  786.9 180.4 %reduce-scatter.23.cloned.1.call-done = f32[2,184,896]{2,1,0:T(8,128)} async-done(((f32[2,1472,896]{2,1,0:T(8,128)}), f32[2,184,896]{2,1,0:T(8,128)}) %reduce-scatter.23.cloned.1.call-update) | async-done | bytes 1318928 | tf_op jit(solution)/shard_map/reduce_scatter | solution.py:281
  972.0 31.2 %all-reduce.9.cloned.1.call-done = (bf16[3,184,384]{2,1,0:T(8,128)(2,1)}, bf16[384,184]{0,1:T(8,128)(2,1)}) async-done(((bf16[3,184,384]{2,1,0:T(8,128)(2,1)}, bf16[384,184]{0,1:T(8,128)(2,1)}), (bf16[3,184,384]{2,1,0:T(8,128)(2,1)}, bf16[384,184]{0,1:T(8,128)(2,1)})) %all-reduce.9.cloned.1.call-update) | async-done | bytes 565264 | tf_op jit(solution)/shard_map/psum | solution.py:285
  1012.3 39.8 %all-reduce.5 = (f32[32,6]{0,1:T(8,128)S(1)}, f32[9]{0:T(128)S(1)}, f32[9]{0:T(128)S(1)}) all-reduce(f32[32,6]{0,1:T(8,128)S(1)} %copy-done.52, f32[9]{0:T(128)S(1)} %concatenate.42, f32[9]{0:T(128)S(1)} %concatenate.44), channel_id=1, replica_groups=mesh['dp'=8,'mp'=4] {'dp','mp'}, use_global_device_ids=true, to_apply=%region_34.35 | all-reduce | flops 210 | bytes 1680 | tf_op jit(solution)/shard_map/psum | solution.py:272
  (264 shorter events, 194.6 us)
Async XLA Ops:
  7.2 69.7 %all-gather.8.cloned.1.call-start = ((), (), s32[]{:S(2)}) async-start(), calls=%async_computation.8 | async-start | bytes 3815424 | tf_op jit(solution)/shard_map/all_gather | solution.py:123
  9.4 109.7 %all-gather.10.cloned.1.call-start = ((), (), s32[]{:S(2)}) async-start(), calls=%async_computation.9 | async-start | bytes 1271808 | tf_op jit(solution)/shard_map/all_gather | solution.py:124
  10.1 197.2 %all-gather.14.cloned.1.call-start = ((), (), s32[]{:S(2)}) async-start(), calls=%async_computation.11 | async-start | bytes 5935104 | tf_op jit(solution)/shard_map/all_gather | solution.py:125
  11.1 220.5 %all-gather.12.cloned.1.call-start = ((), (), s32[]{:S(2)}) async-start(), calls=%async_computation.10 | async-start | bytes 2949120 | tf_op jit(solution)/shard_map/all_gather | solution.py:183
  123.3 134.4 %all-gather.18.cloned.1.call-start = ((), (), s32[]{:S(2)}) async-start(), calls=%async_computation.14 | async-start | bytes 2949120 | tf_op jit(solution)/shard_map/all_gather | solution.py:199
  126.1 189.2 %all-gather.16.cloned.1.call-start = ((), (), s32[]{:S(2)}) async-start(), calls=%async_computation.12 | async-start | bytes 2967552 | tf_op jit(solution)/shard_map/all_gather | solution.py:126
  128.0 254.8 %reduce-scatter.19.cloned.1.call-start = ((), (), s32[]{:S(2)}) async-start(), calls=%async_computation.15 | async-start | bytes 5898240 | tf_op jit(solution)/shard_map/reduce_scatter | solution.py:208
  336.3 82.4 %reduce-scatter.17.cloned.1.call-start = ((), (), s32[]{:S(2)}) async-start(), calls=%async_computation.13 | async-start | bytes 2949120 | tf_op jit(solution)/shard_map/reduce_scatter | solution.py:189
  342.6 110.1 %reduce-scatter.27.cloned.1.call-start = ((), (), s32[]{:S(2)}) async-start(), calls=%async_computation.19 | async-start | bytes 737280
  430.5 47.3 %reduce-scatter.25.cloned.1.call-start = ((), (), s32[]{:S(2)}) async-start(), calls=%async_computation.18 | async-start | bytes 737280
  436.4 148.7 %reduce-scatter.31.cloned.1.call-start = ((), (), s32[]{:S(2)}) async-start(), calls=%async_computation.21 | async-start | bytes 5935104
  443.1 213.6 %reduce-scatter.29.cloned.1.call-start = ((), (), s32[]{:S(2)}) async-start(), calls=%async_computation.20 | async-start | bytes 2543616
  446.4 338.5 %reduce-scatter.21.cloned.1.call-start = ((), (), s32[]{:S(2)}) async-start(), calls=%async_computation.16 | async-start | bytes 7630848 | tf_op jit(solution)/shard_map/reduce_scatter | solution.py:279
  484.4 482.9 %reduce-scatter.23.cloned.1.call-start = ((), (), s32[]{:S(2)}) async-start(), calls=%async_computation.17 | async-start | bytes 11870208 | tf_op jit(solution)/shard_map/reduce_scatter | solution.py:281
  496.6 506.6 %all-reduce.9.cloned.1.call-start = ((), (), s32[]{:S(2)}) async-start(), calls=%async_computation.22 | async-start | bytes 1130496 | tf_op jit(solution)/shard_map/psum | solution.py:285
  531.6 45.7 %copy-start.45 = (f32[192]{0:T(256)S(1)}, f32[192]{0:T(256)}, u32[]{:S(2)}) copy-start(f32[192]{0:T(256)} %copy-done.44) | copy-start | bytes 2308
  588.4 473.8 %copy-start.18 = (f32[896,184]{0,1:T(8,128)}, f32[896,184]{0,1:T(8,128)S(1)}, u32[]{:S(2)}) copy-start(f32[896,184]{0,1:T(8,128)S(1)} %get-tuple-element.66) | copy-start | bytes 1978372
  588.4 379.0 %copy-start.8 = (f32[2,184,896]{2,1,0:T(8,128)S(1)}, f32[2,184,896]{2,1,0:T(8,128)}, u32[]{:S(2)}) copy-start(f32[2,184,896]{2,1,0:T(8,128)} %param.26) | copy-start | bytes 3956740
  786.9 216.3 %copy-start.21 = (f32[384,184]{0,1:T(8,128)S(1)}, f32[384,184]{0,1:T(8,128)}, u32[]{:S(2)}) copy-start(f32[384,184]{0,1:T(8,128)} %param.25) | copy-start | bytes 847876
  786.9 216.3 %copy-start.30 = (f32[384,184]{0,1:T(8,128)S(1)}, f32[384,184]{0,1:T(8,128)}, u32[]{:S(2)}) copy-start(f32[384,184]{0,1:T(8,128)} %param.31) | copy-start | bytes 847876
  1007.3 44.9 %copy-start.40 = (f32[32,6]{0,1:T(8,128)S(1)}, f32[32,6]{0,1:T(8,128)}, u32[]{:S(2)}) copy-start(f32[32,6]{0,1:T(8,128)} %param.29) | copy-start | bytes 2308
  1007.3 44.9 %copy-start.50 = (f32[32,6]{0,1:T(8,128)S(1)}, f32[32,6]{0,1:T(8,128)}, u32[]{:S(2)}) copy-start(f32[32,6]{0,1:T(8,128)} %param.35) | copy-start | bytes 2308
  1007.3 51.5 %copy-start.49 = (f32[2,184]{1,0:T(2,128)S(1)}, f32[2,184]{1,0:T(2,128)}, u32[]{:S(2)}) copy-start(f32[2,184]{1,0:T(2,128)} %get-tuple-element.63) | copy-start | bytes 4420
  1010.8 51.4 %copy-start.12 = (f32[896,184]{0,1:T(8,128)S(1)}, f32[896,184]{0,1:T(8,128)}, u32[]{:S(2)}) copy-start(f32[896,184]{0,1:T(8,128)} %param.27) | copy-start | bytes 1978372
  (58 other events, 462.9 us)
Sparse Core Ops, SparseCore 0:
  10.9 66.0 all-gather.7
  79.7 39.2 all-gather.9
  121.8 85.4 all-gather.13
  209.3 22.2 all-gather.11
  233.6 24.0 all-gather.17
  260.4 54.8 all-gather.15
  336.4 46.4 reduce-scatter.18
  385.5 33.0 reduce-scatter.16
  430.6 22.0 reduce-scatter.26
  455.7 22.0 reduce-scatter.24
  481.3 103.7 reduce-scatter.30
  589.0 67.6 reduce-scatter.28
  660.4 124.5 reduce-scatter.20
  788.7 178.6 reduce-scatter.22
  970.8 32.4 all-reduce.8
where the time goes:
time: 1080 us; the launch traced here: 1070 us
  waiting for transfers between devices  697 us (65%)
  blocking collectives  119 us (11%)
  matrix products  89.8 us (8%)
  other arithmetic  71.5 us (7%)
  local copies, waits for them, and re-layouts  66.1 us (6%)
  between operations  19.6 us (2%)
  starting transfers between devices  12.3 us (1%)
    reduce_scatter x1, waiting for transfers between devices, shards(): lax.psum_scatter(grad_expand_in, 'dp', scatter_dimension=1, tiled=True)  180 us
    reduce_scatter x1, waiting for transfers between devices, shards(): lax.psum_scatter(grad_heads_in, 'dp', scatter_dimension=1, tiled=True)  127 us
    unnamed x19, waiting for transfers between devices  96.1 us
    psum x2, blocking collectives, shards(): lax.psum((jnp.stack([gain_one_grad, gain_two_grad]), grad_table), ('dp',...  81.2 us
    all_gather x1, waiting for transfers between devices, shards(): lax.all_gather(expand_in.astype(jnp.bfloat16), 'dp', axis=1, tiled=True)  79.3 us
    all_gather x1, waiting for transfers between devices, shards(): lax.all_gather(expand_out.astype(jnp.bfloat16), 'dp', axis=1, tiled=True)  57.5 us
    reduce_scatter x1, waiting for transfers between devices, shards(): lax.psum_scatter(jnp.dot(hidden_part, full_back, preferred_element_type=j...  32.7 us
    psum x1, waiting for transfers between devices, shards(): lax.psum(head_in_part.astype(jnp.bfloat16), 'mp').astype(jnp.float32)  31.2 us
  transfers between devices with their start and end apart: 15, of which 15 were waited for; matrix products, arithmetic and copies ran while one was open for 15% of the time, Pallas kernels for 0%

commit v1 on v0

v1 whole, which is shorter than its diff:
```python
from functools import partial

import jax
import jax.numpy as jnp
from jax import lax
from jax.experimental import pallas as pl
from jax.experimental.pallas import tpu as pltpu
from jax.sharding import PartitionSpec as P

HEADS = 6
HEAD_DIM = 64
STEP = 10
INNER = 384
LANES = 128
PAIRS = INNER // LANES
MESH = pl.DeviceIdType.MESH
VMEM_BYTES = 56 * 2**20
RING_LIMIT = 8


norm_eps = 1e-06
beta_first = 0.9
beta_second = 0.999
adam_eps = 1e-06
weight_decay = 0.01
learn_rate = 0.4
masked_fill = -1000000000.0
bucket_edges = (12, 16, 23, 32, 46, 64, 91)
highest = lax.Precision.HIGHEST
f32 = jnp.float32
bf16 = jnp.bfloat16


def bucket_ids(offsets):
    distance = jnp.abs(offsets)
    coarse = jnp.full_like(distance, 8)
    for edge_value in bucket_edges:
        coarse = coarse + (distance >= edge_value).astype(jnp.int32)
    nearby = jnp.where(distance < 8, distance, coarse)
    return nearby + 16 * (offsets > 0).astype(jnp.int32)


def rms_scale(hidden_rows, gain_vector):
    return (
        hidden_rows
        * lax.rsqrt(jnp.mean(hidden_rows * hidden_rows, axis=-1, keepdims=True) + norm_eps)
        * gain_vector
    )


def contract_rows(left_side, right_side):
    return lax.dot_general(
        left_side, right_side, (((0,), (0,)), ((), ())), preferred_element_type=f32
    )


def contract_cols(left_side, right_side):
    return lax.dot_general(
        left_side, right_side, (((1,), (1,)), ((), ())), preferred_element_type=f32
    )


def matmul(left_side, right_side):
    return jnp.dot(left_side, right_side, preferred_element_type=f32)


def ring_order(size):
    return list(range(0, size, 2)) + list(range(size - 1, 0, -2))


def ring_pairs(size):
    order = ring_order(size)
    forward = [(order[spot], order[(spot + 1) % size]) for spot in range(size)]
    return forward, [(target, source) for source, target in forward]


def ring_owner(spot, size):
    late = (spot >= size // 2).astype(jnp.int32)
    return 2 * spot + late * (2 * size - 1 - 4 * spot)


def ring_spot(index, size):
    return index // 2 + lax.rem(index, 2) * (size - 1 - 2 * (index // 2))


def cut_of(width):
    return ((width // LANES + 1) // 2) * LANES


def assemble_kernel(size, cut, *refs):
    slabs, (left, right, out, sems) = refs[:-4], refs[-4:]
    spot = ring_spot(lax.axis_index("dp"), size)
    copies = []
    for number, slab in enumerate(slabs):
        shift = number if number < size // 2 else number + 1
        owner = ring_owner(lax.rem(spot + shift, size), size)
        copies.append(pltpu.make_async_copy(slab, out.at[:, owner], sems.at[number]))
    owner = ring_owner(lax.rem(spot + size // 2, size), size)
    width = out.shape[-1]
    copies.append(
        pltpu.make_async_copy(left, out.at[:, owner, :, pl.ds(0, cut)], sems.at[size - 1])
    )
    copies.append(
        pltpu.make_async_copy(right, out.at[:, owner, :, pl.ds(cut, width - cut)], sems.at[size])
    )
    for copy in copies:
        copy.start()
    for copy in copies:
        copy.wait()


def gather_dp(part):
    size = lax.axis_size("dp")
    if size > RING_LIMIT:
        return lax.all_gather(part, "dp", axis=1, tiled=True)
    forward, backward = ring_pairs(size)
    count, rows, width = part.shape
    cut = cut_of(width)
    slabs = [None] * size
    slabs[0] = ahead = behind = part
    for hop in range(1, size // 2):
        ahead = lax.ppermute(ahead, "dp", forward)
        behind = lax.ppermute(behind, "dp", backward)
        slabs[size - hop] = ahead
        slabs[hop] = behind
    left = lax.ppermute(ahead[..., :cut], "dp", forward)
    right = lax.ppermute(behind[..., cut:], "dp", backward)
    operands = [slab for slab in slabs if slab is not None] + [left, right]
    total = count * size * rows * width * part.dtype.itemsize
    whole = pl.pallas_call(
        partial(assemble_kernel, size, cut),
        out_shape=jax.ShapeDtypeStruct((count, size, rows, width), part.dtype),
        in_specs=[pl.BlockSpec(memory_space=pl.ANY)] * len(operands),
        out_specs=pl.BlockSpec(memory_space=pltpu.VMEM),
        scratch_shapes=[pltpu.SemaphoreType.DMA((size + 1,))],
        compiler_params=pltpu.CompilerParams(vmem_limit_bytes=VMEM_BYTES),
        cost_estimate=pl.CostEstimate(flops=0, bytes_accessed=2 * total, transcendentals=0),
        name="assemble",
    )(*operands)
    return whole.reshape(count, size * rows, width)


def scatter_dp(whole):
    size = lax.axis_size("dp")
    if size > RING_LIMIT:
        return lax.psum_scatter(whole.astype(f32), "dp", scatter_dimension=1, tiled=True)
    forward, backward = ring_pairs(size)
    count, depth, width = whole.shape
    rows = depth // size
    cut = cut_of(width)
    spot = ring_spot(lax.axis_index("dp"), size)

    def term(shift):
        owner = ring_owner(lax.rem(spot + size + shift, size), size)
        return lax.dynamic_slice_in_dim(whole, owner * rows, rows, axis=1)

    far = term(size // 2)
    ahead = lax.ppermute(far[..., :cut], "dp", forward)
    behind = lax.ppermute(far[..., cut:], "dp", backward)
    for hop in range(size // 2 - 1, 0, -1):
        mine = term(hop).astype(f32)
        other = term(-hop).astype(f32)
        if hop == size // 2 - 1:
            ahead = jnp.concatenate([mine[..., :cut] + ahead.astype(f32), mine[..., cut:]], -1)
            behind = jnp.concatenate([other[..., :cut], other[..., cut:] + behind.astype(f32)], -1)
        else:
            ahead = mine + ahead.astype(f32)
            behind = other + behind.astype(f32)
        ahead = lax.ppermute(ahead.astype(bf16), "dp", forward)
        behind = lax.ppermute(behind.astype(bf16), "dp", backward)
    return term(0).astype(f32) + ahead.astype(f32) + behind.astype(f32)


def swap(part, bit):
    size = lax.axis_size("mp")
    return lax.ppermute(part, "mp", [(index, index ^ bit) for index in range(size)])


def gather_mp(part):
    across = swap(part, 2)
    beside = swap(part, 1)
    return part, across, beside, swap(across, 1)


def offset_values(table_ref, first_row, rows, span):
    offsets = lax.broadcasted_iota(jnp.int32, (8, span), 1) - (rows - 1) - first_row
    buckets = bucket_ids(offsets)
    table = table_ref[...]
    values = jnp.zeros((8, span), f32)
    for number in range(table.shape[1]):
        values = jnp.where(buckets == number, table[:, number : number + 1], values)
    return values


def segments_at(positions, first_len, second_len):
    return (positions >= first_len).astype(jnp.int32) + (
        positions >= first_len + second_len
    ).astype(jnp.int32)


def allowed_pairs(lens_ref, first_row, rows, keys):
    query = segments_at(
        first_row + lax.broadcasted_iota(jnp.int32, (rows, 1), 0), lens_ref[0, 0], lens_ref[0, 1]
    )
    key = segments_at(
        lax.broadcasted_iota(jnp.int32, (1, keys), 1), lens_ref[0, 0], lens_ref[0, 1]
    )
    return query == key


def skewed_bias(values, head, rows, keys, span):
    wide = jnp.broadcast_to(values[head : head + 1, :], (rows, span))
    return pltpu.roll(wide, span - (rows - 1), 1, stride=1, stride_axis=0)[:, :keys]


def forward_kernel(
    span,
    lens_ref,
    own_ref,
    across_ref,
    beside_ref,
    corner_ref,
    heads_ref,
    table_ref,
    tokens_ref,
    gain_ref,
    mixed_ref,
    query_ref,
    key_ref,
    value_ref,
    log_ref,
    residual_ref,
    normed_ref,
):
    rows = own_ref.shape[0]
    keys = key_ref.shape[0]
    spot = lax.axis_index("mp")
    first_row = spot * rows
    for block_ref, bit in ((own_ref, 0), (across_ref, 2), (beside_ref, 1), (corner_ref, 3)):
        place = pl.ds(pl.multiple_of((spot ^ bit) * rows, rows), rows)
        block = block_ref[...]
        key_ref[place, :] = matmul(block, heads_ref[1]).astype(bf16)
        value_ref[place, :] = matmul(block, heads_ref[2]).astype(bf16)
    query_ref[...] = matmul(own_ref[...], heads_ref[0]).astype(bf16)
    values = offset_values(table_ref, first_row, rows, span)
    allowed = allowed_pairs(lens_ref, first_row, rows, keys)
    lane = lax.broadcasted_iota(jnp.int32, (1, LANES), 1)
    logs = jnp.zeros((rows, LANES), f32)
    for pair in range(PAIRS):
        part = slice(pair * LANES, (pair + 1) * LANES)
        query = query_ref[:, part]
        key = key_ref[:, part]
        value = value_ref[:, part]
        mixed = jnp.zeros((rows, LANES), f32)
        for half in range(2):
            head = 2 * pair + half
            mask = (lane // HEAD_DIM) == half
            scores = contract_cols(jnp.where(mask, query, jnp.zeros_like(query)), key)
            scores = jnp.where(
                allowed, scores + skewed_bias(values, head, rows, keys, span), masked_fill
            )
            top = jnp.max(scores, axis=-1, keepdims=True)
            powers = jnp.exp(scores - top)
            total = jnp.sum(powers, axis=-1, keepdims=True)
            soft = (powers * (1.0 / total)).astype(bf16)
            mixed = jnp.where(mask, matmul(soft, value), mixed)
            logs = jnp.where(lane == head, top + jnp.log(total), logs)
        mixed_ref[:, part] = mixed.astype(bf16)
    log_ref[...] = logs
    residual = tokens_ref[...].astype(f32) + contract_cols(mixed_ref[...], heads_ref[3])
    residual_ref[...] = residual
    normed_ref[...] = rms_scale(residual, gain_ref[...]).astype(bf16)


def norm_backward(rows_in, gain, grad):
    scale = lax.rsqrt(jnp.mean(rows_in * rows_in, axis=-1, keepdims=True) + norm_eps)
    unit = rows_in * scale
    inner = grad * gain
    out = scale * (inner - unit * jnp.mean(inner * unit, axis=-1, keepdims=True))
    return out, jnp.sum(grad * unit, axis=0, keepdims=True)


def backward_kernel(
    span,
    lens_ref,
    part_ref,
    across_ref,
    residual_ref,
    upstream_ref,
    gain_ref,
    heads_ref,
    query_ref,
    key_ref,
    value_ref,
    log_ref,
    table_ref,
    residual_grad_ref,
    attended_ref,
    query_grad_ref,
    near_ref,
    far_ref,
    offset_ref,
    gain_grad_ref,
    whole_ref,
):
    rows = query_ref.shape[0]
    keys = key_ref.shape[0]
    spot = lax.axis_index("mp")
    first_row = spot * rows
    grad = part_ref[...].astype(f32) + across_ref[...].astype(f32)
    through, gain_grad = norm_backward(residual_ref[...], gain_ref[...], grad)
    gain_grad_ref[...] = gain_grad
    residual_grad = upstream_ref[...].astype(f32) + through
    residual_grad_ref[...] = residual_grad
    attended = residual_grad.astype(bf16)
    attended_ref[...] = attended
    mixed_grad_all = matmul(attended, heads_ref[3]).astype(bf16)
    values = offset_values(table_ref, first_row, rows, span)
    allowed = allowed_pairs(lens_ref, first_row, rows, keys)
    lane = lax.broadcasted_iota(jnp.int32, (1, LANES), 1)
    flip = (
        lax.broadcasted_iota(jnp.int32, (rows, rows), 0)
        + lax.broadcasted_iota(jnp.int32, (rows, rows), 1)
        == rows - 1
    ).astype(bf16)
    for pair in range(PAIRS):
        part = slice(pair * LANES, (pair + 1) * LANES)
        query = query_ref[:, part]
        key = key_ref[:, part]
        value = value_ref[:, part]
        mixed_grad = mixed_grad_all[:, part]
        query_grad = jnp.zeros((rows, LANES), f32)
        key_grad = jnp.zeros((keys, LANES), f32)
        value_grad = jnp.zeros((keys, LANES), f32)
        for half in range(2):
            head = 2 * pair + half
            mask = (lane // HEAD_DIM) == half
            query_own = jnp.where(mask, query, jnp.zeros_like(query))
            mixed_own = jnp.where(mask, mixed_grad, jnp.zeros_like(mixed_grad))
            scores = contract_cols(query_own, key)
            scores = jnp.where(
                allowed, scores + skewed_bias(values, head, rows, keys, span), masked_fill
            )
            soft = jnp.exp(scores - log_ref[:, head : head + 1])
            soft_grad = contract_cols(mixed_own, value)
            corr = jnp.sum(soft * soft_grad, axis=-1, keepdims=True)
            scores_grad = (soft * (soft_grad - corr)).astype(bf16)
            query_grad = jnp.where(mask, matmul(scores_grad, key), query_grad)
            key_grad = key_grad + contract_rows(scores_grad, query_own)
            value_grad = value_grad + contract_rows(soft.astype(bf16), mixed_own)
            flipped = matmul(flip, scores_grad)
            flipped = jnp.concatenate([flipped, jnp.zeros((rows, span - keys), f32)], axis=1)
            skewed = pltpu.roll(flipped, 0, 1, stride=1, stride_axis=0)
            offset_ref[head : head + 1, :] = jnp.sum(skewed, axis=0, keepdims=True)
        query_grad_ref[:, part] = query_grad.astype(bf16)
        whole_ref[:, part] = key_grad
        whole_ref[:, INNER + pair * LANES : INNER + (pair + 1) * LANES] = value_grad
    offset_ref[HEADS:, :] = jnp.zeros((8 - HEADS, span), f32)
    for number, bit in enumerate((0, 2)):
        place = pl.ds(pl.multiple_of((spot ^ bit) * rows, rows), rows)
        near_ref[number * rows : (number + 1) * rows, :] = whole_ref[place, :]
    for number, bit in enumerate((1, 3)):
        place = pl.ds(pl.multiple_of((spot ^ bit) * rows, rows), rows)
        far_ref[number * rows : (number + 1) * rows, :] = whole_ref[place, :].astype(bf16)


def input_kernel(
    own_ref,
    beside_ref,
    across_ref,
    query_grad_ref,
    heads_ref,
    tokens_ref,
    gain_ref,
    residual_grad_ref,
    tokens_grad_ref,
    both_ref,
    gain_grad_ref,
):
    rows = query_grad_ref.shape[0]
    both = (
        own_ref[:rows, :]
        + beside_ref[:rows, :].astype(f32)
        + across_ref[...].astype(f32)
    ).astype(bf16)
    both_ref[...] = both
    grad = (
        contract_cols(query_grad_ref[...], heads_ref[0])
        + contract_cols(both[:, :INNER], heads_ref[1])
        + contract_cols(both[:, INNER:], heads_ref[2])
    )
    through, gain_grad = norm_backward(tokens_ref[...].astype(f32), gain_ref[...], grad)
    gain_grad_ref[...] = gain_grad
    tokens_grad_ref[...] = residual_grad_ref[...] + through


def vmem_call(body, outs, cost, scratch=(), name=None, smem_first=False):
    def run(*operands):
        specs = [pl.BlockSpec(memory_space=pltpu.VMEM)] * len(operands)
        if smem_first:
            specs[0] = pl.BlockSpec(memory_space=pltpu.SMEM)
        return pl.pallas_call(
            body,
            out_shape=[jax.ShapeDtypeStruct(shape, kind) for shape, kind in outs],
            in_specs=specs,
            out_specs=[pl.BlockSpec(memory_space=pltpu.VMEM)] * len(outs),
            scratch_shapes=list(scratch),
            compiler_params=pltpu.CompilerParams(vmem_limit_bytes=VMEM_BYTES),
            cost_estimate=pl.CostEstimate(
                flops=cost[0], bytes_accessed=cost[1], transcendentals=cost[2]
            ),
            name=name,
        )(*operands)

    return run


def total_kernel(sizes, part_ref, out_ref, line_ref, plane_ref, line_send, line_recv, plane_send, plane_recv):
    plane, line = sizes
    dp_spot, mp_spot = lax.axis_index("dp"), lax.axis_index("mp")
    barrier = pltpu.get_barrier_semaphore()
    for step in range(1, line):
        pl.semaphore_signal(
            barrier, 1, device_id=(dp_spot, lax.rem(mp_spot + step, line)), device_id_type=MESH
        )
    for step in range(1, plane):
        pl.semaphore_signal(
            barrier, 1, device_id=(lax.rem(dp_spot + step, plane), mp_spot), device_id_type=MESH
        )
    pl.semaphore_wait(barrier, line + plane - 2)

    def exchange(source, slots, size, spot, send, recv, target):
        slots[spot] = source[...]
        copies = [
            pltpu.make_async_remote_copy(
                src_ref=source,
                dst_ref=slots.at[spot],
                send_sem=send.at[step],
                recv_sem=recv.at[step],
                device_id=target(lax.rem(spot + step, size)),
                device_id_type=MESH,
            )
            for step in range(1, size)
        ]
        for copy in copies:
            copy.start()
        for copy in copies:
            copy.wait()
        total = slots[0]
        for index in range(1, size):
            total = total + slots[index]
        out_ref[...] = total

    exchange(part_ref, line_ref, line, mp_spot, line_send, line_recv, lambda to: (dp_spot, to))
    exchange(out_ref, plane_ref, plane, dp_spot, plane_send, plane_recv, lambda to: (to, mp_spot))


def total_all(part, number):
    plane, line = lax.axis_size("dp"), lax.axis_size("mp")
    if plane > RING_LIMIT:
        return lax.psum(part, ("dp", "mp"))
    return pl.pallas_call(
        partial(total_kernel, (plane, line)),
        out_shape=jax.ShapeDtypeStruct(part.shape, part.dtype),
        in_specs=[pl.BlockSpec(memory_space=pltpu.VMEM)],
        out_specs=pl.BlockSpec(memory_space=pltpu.VMEM),
        scratch_shapes=[
            pltpu.VMEM((line,) + part.shape, f32),
            pltpu.VMEM((plane,) + part.shape, f32),
            pltpu.SemaphoreType.DMA((line,)),
            pltpu.SemaphoreType.DMA((line,)),
            pltpu.SemaphoreType.DMA((plane,)),
            pltpu.SemaphoreType.DMA((plane,)),
        ],
        compiler_params=pltpu.CompilerParams(collective_id=number, has_side_effects=True),
        name="total",
    )(part)


def small_gather_kernel(size, part_ref, out_ref, send, recv):
    dp_spot, mp_spot = lax.axis_index("dp"), lax.axis_index("mp")
    barrier = pltpu.get_barrier_semaphore()
    for step in range(1, size):
        pl.semaphore_signal(
            barrier, 1, device_id=(lax.rem(dp_spot + step, size), mp_spot), device_id_type=MESH
        )
    pl.semaphore_wait(barrier, size - 1)
    out_ref[dp_spot] = part_ref[...]
    copies = [
        pltpu.make_async_remote_copy(
            src_ref=part_ref,
            dst_ref=out_ref.at[dp_spot],
            send_sem=send.at[step],
            recv_sem=recv.at[step],
            device_id=(lax.rem(dp_spot + step, size), mp_spot),
            device_id_type=MESH,
        )
        for step in range(1, size)
    ]
    for copy in copies:
        copy.start()
    for copy in copies:
        copy.wait()


def gather_gains(gains):
    size = lax.axis_size("dp")
    if size > RING_LIMIT:
        return lax.all_gather(gains, "dp", axis=1, tiled=True)
    count, width = gains.shape
    wide = -(-width // LANES) * LANES
    part = jnp.pad(gains, ((0, 8 - count), (0, wide - width)))
    whole = pl.pallas_call(
        partial(small_gather_kernel, size),
        out_shape=jax.ShapeDtypeStruct((size,) + part.shape, part.dtype),
        in_specs=[pl.BlockSpec(memory_space=pltpu.VMEM)],
        out_specs=pl.BlockSpec(memory_space=pltpu.VMEM),
        scratch_shapes=[pltpu.SemaphoreType.DMA((size,)), pltpu.SemaphoreType.DMA((size,))],
        compiler_params=pltpu.CompilerParams(collective_id=3, has_side_effects=True),
        name="gather_gains",
    )(part)
    return jnp.concatenate([whole[index, :count, :width] for index in range(size)], axis=1)


def pack_rows(parts):
    flat = jnp.concatenate([part.reshape(-1) for part in parts])
    count = -(-flat.shape[0] // (8 * LANES)) * 8
    return jnp.pad(flat, (0, count * LANES - flat.shape[0])).reshape(count, LANES)


def lamb_parts(weight, gradient, first_moment, second, decay_rate):
    new_first = beta_first * first_moment + (1.0 - beta_first) * gradient
    new_second = beta_second * second + (1.0 - beta_second) * gradient * gradient
    first_fix = 1.0 - beta_first**STEP
    second_fix = 1.0 - beta_second**STEP
    step_dir = (
        new_first / first_fix / (jnp.sqrt(new_second / second_fix) + adam_eps) + decay_rate * weight
    )
    return (new_first, new_second, step_dir)


def sub_squares(values, sub_count):
    flat_values = values.reshape(sub_count, -1)
    return jnp.sum(flat_values * flat_values, axis=1)


def shards(
    tokens,
    cotangent,
    lengths,
    heads_in,
    heads_out,
    expand_in,
    expand_out,
    norm_gains,
    bias_table,
    heads_in_first,
    heads_out_first,
    expand_in_first,
    expand_out_first,
    gains_first,
    table_first,
    heads_in_second,
    heads_out_second,
    expand_in_second,
    expand_out_second,
    gains_second,
    table_second,
):
    rows, depth = tokens.shape
    mp_size = lax.axis_size("mp")
    mp_spot = lax.axis_index("mp")
    keys = rows * mp_size
    span = -(-(keys + rows - 1) // LANES) * LANES
    first_row = mp_spot * rows
    shard_width = norm_gains.shape[1]
    buckets = bias_table.shape[0]

    four = jnp.concatenate([heads_in, heads_out.T[None]], axis=0).astype(bf16)
    mine = lax.dynamic_slice_in_dim(four, mp_spot, 1, axis=0)
    mine_all = gather_dp(mine)
    full_gains = gather_gains(norm_gains.astype(bf16).astype(f32))
    gain_one, gain_two = full_gains[0:1], full_gains[1:2]
    inputs = tokens.astype(f32)
    normed = rms_scale(inputs, gain_one).astype(bf16)
    normed_parts = gather_mp(normed)
    used = first_row + jnp.arange(rows, dtype=jnp.int32) < lengths[0, 0] + lengths[0, 1]
    upstream = jnp.where(used[:, None], cotangent, jnp.zeros_like(cotangent))
    upstream_parts = gather_mp(upstream)

    mine_parts = gather_mp(mine_all)
    by_bit = jnp.concatenate([mine_parts[0], mine_parts[2], mine_parts[1], mine_parts[3]], axis=0)
    full_heads = jnp.concatenate(
        [lax.dynamic_slice_in_dim(by_bit, mp_spot ^ number, 1, axis=0) for number in range(mp_size)],
        axis=0,
    )
    wide_in = gather_dp(expand_in.astype(bf16))
    wide_out = gather_dp(expand_out.T.astype(bf16)[None])[0]

    table = jnp.pad(bias_table.T, ((0, 8 - HEADS), (0, 0)))
    attention_flops = rows * keys * LANES * HEADS
    mixed, query, key, value, logs, residual, normed_two = vmem_call(
        partial(forward_kernel, span),
        [
            ((rows, INNER), bf16),
            ((rows, INNER), bf16),
            ((keys, INNER), bf16),
            ((keys, INNER), bf16),
            ((rows, LANES), f32),
            ((rows, depth), f32),
            ((rows, depth), bf16),
        ],
        (
            2 * depth * INNER * (2 * keys + 2 * rows) + 4 * attention_flops,
            2 * (4 * depth * INNER + 2 * keys * depth),
            rows * keys * HEADS,
        ),
        name="attention_forward",
        smem_first=True,
    )(lengths, *normed_parts, full_heads, table, tokens, gain_two)

    normed_all = jnp.concatenate(gather_mp(normed_two), axis=0)
    upstream_all = jnp.concatenate(upstream_parts, axis=0)
    gate_pre = matmul(normed_all, wide_in[0])
    up_pre = matmul(normed_all, wide_in[1])
    gelu_gate, gelu_pull = jax.vjp(partial(jax.nn.gelu, approximate=True), gate_pre)
    hidden = (gelu_gate * up_pre).astype(bf16)
    expand_out_grad = scatter_dp(contract_rows(upstream_all, hidden).astype(bf16)[None])[0].T
    feed_part = contract_cols(hidden, wide_out).astype(bf16)
    feed_near = feed_part[: 2 * rows].astype(f32) + swap(feed_part[2 * rows :], 1).astype(f32)
    feed_out = feed_near[:rows] + swap(feed_near[rows:].astype(bf16), 2).astype(f32)
    layer_out = (residual + feed_out).astype(bf16)

    hidden_grad = matmul(upstream_all, wide_out)
    up_grad = (hidden_grad * gelu_gate).astype(bf16)
    gate_grad = gelu_pull(hidden_grad * up_pre)[0].astype(bf16)
    normed_part = contract_cols(gate_grad, wide_in[0]) + contract_cols(up_grad, wide_in[1])
    normed_near = normed_part[: 2 * rows] + swap(normed_part[2 * rows :].astype(bf16), 1).astype(f32)
    normed_across = swap(normed_near[rows:].astype(bf16), 2)
    expand_in_grad = scatter_dp(
        jnp.stack(
            [
                contract_rows(normed_all, gate_grad).astype(bf16),
                contract_rows(normed_all, up_grad).astype(bf16),
            ]
        )
    )

    residual_grad, attended_grad, query_grad, near, far, offset_grad, gain_two_grad = vmem_call(
        partial(backward_kernel, span),
        [
            ((rows, depth), f32),
            ((rows, depth), bf16),
            ((rows, INNER), bf16),
            ((2 * rows, 2 * INNER), f32),
            ((2 * rows, 2 * INNER), bf16),
            ((8, span), f32),
            ((1, depth), f32),
        ],
        (
            2 * depth * INNER * rows + 10 * attention_flops,
            rows * depth * 16 + 2 * (4 * depth * INNER + 2 * keys * INNER),
            rows * keys * HEADS,
        ),
        scratch=[pltpu.VMEM((keys, 2 * INNER), f32)],
        name="attention_backward",
        smem_first=True,
    )(
        lengths,
        normed_near[:rows],
        normed_across,
        residual,
        upstream,
        gain_two,
        full_heads,
        query,
        key,
        value,
        logs,
        table,
    )
    attended_parts = gather_mp(attended_grad)
    beside = swap(far, 1)
    across = swap((near[rows:] + beside[rows:].astype(f32)).astype(bf16), 2)
    tokens_grad, both, gain_one_grad = vmem_call(
        input_kernel,
        [((rows, depth), f32), ((rows, 2 * INNER), bf16), ((1, depth), f32)],
        (6 * rows * depth * INNER, rows * depth * 14 + 8 * depth * INNER, 0),
        name="input_backward",
    )(near, beside, across, query_grad, full_heads, tokens, gain_one, residual_grad)

    offered = jnp.stack([query_grad, both[:, :INNER], both[:, INNER:], mixed])

    def for_bit(bit):
        return lax.dynamic_slice_in_dim(offered, mp_spot ^ bit, 1, axis=0)

    from_beside = swap(jnp.concatenate([for_bit(1), for_bit(3)], axis=0), 1)
    from_across = swap(jnp.concatenate([for_bit(2), from_beside[1:]], axis=0), 2)
    right = jnp.concatenate(
        [for_bit(0)[0], from_across[0], from_beside[0], from_across[1]], axis=0
    )
    left = jnp.where(
        mp_spot == mp_size - 1,
        jnp.concatenate(attended_parts, axis=0),
        jnp.concatenate(normed_parts, axis=0),
    )
    mine_grad = scatter_dp(contract_rows(left, right).astype(bf16)[None]).astype(bf16)
    grad_parts = gather_mp(mine_grad)
    grads_by_bit = jnp.concatenate(
        [grad_parts[0], grad_parts[2], grad_parts[1], grad_parts[3]], axis=0
    )
    heads_grad = [
        lax.dynamic_slice_in_dim(grads_by_bit, mp_spot ^ number, 1, axis=0)
        for number in range(mp_size)
    ]
    head_in_grad = jnp.concatenate(heads_grad[:3], axis=0).astype(f32)
    head_out_grad = heads_grad[3][0].T.astype(f32)

    reach = jnp.arange(span, dtype=jnp.int32) - (rows - 1) - first_row
    onehot = (bucket_ids(reach)[:, None] == jnp.arange(buckets, dtype=jnp.int32)[None, :]).astype(f32)
    table_part = jnp.dot(offset_grad, onehot, precision=highest)[:HEADS].T
    gain_parts = jnp.concatenate([gain_one_grad, gain_two_grad], axis=0)
    small = total_all(pack_rows([gain_parts, table_part]), 1).reshape(-1)
    gains_total = small[: 2 * depth].reshape(2, depth)
    table_grad = small[2 * depth : 2 * depth + buckets * HEADS].reshape(buckets, HEADS)
    gains_grad = lax.dynamic_slice_in_dim(
        gains_total, lax.axis_index("dp") * shard_width, shard_width, 1
    )

    weight_list = (heads_in, heads_out, expand_in, expand_out, norm_gains, bias_table)
    grad_list = (
        head_in_grad,
        head_out_grad,
        expand_in_grad,
        expand_out_grad,
        gains_grad,
        table_grad,
    )
    first_list = (
        heads_in_first,
        heads_out_first,
        expand_in_first,
        expand_out_first,
        gains_first,
        table_first,
    )
    second_list = (
        heads_in_second,
        heads_out_second,
        expand_in_second,
        expand_out_second,
        gains_second,
        table_second,
    )
    decay_list = (weight_decay, weight_decay, weight_decay, weight_decay, 0.0, 0.0)
    sub_list = (3, 1, 2, 1, 2, 1)
    results = [
        lamb_parts(
            weight_list[number],
            grad_list[number],
            first_list[number],
            second_list[number],
            decay_list[number],
        )
        for number in range(6)
    ]
    shared_scale = 1.0 / mp_size
    share_list = (shared_scale, shared_scale, 1.0, 1.0, shared_scale)
    weight_sq = [sub_squares(weight_list[number], sub_list[number]) for number in range(6)]
    step_sq = [sub_squares(results[number][2], sub_list[number]) for number in range(6)]
    sums = total_all(
        pack_rows(
            [weight_sq[number] * share_list[number] for number in range(5)]
            + [step_sq[number] * share_list[number] for number in range(5)]
        ),
        2,
    )[0]
    count = sum(sub_list[:5])
    weight_norm = jnp.sqrt(jnp.concatenate([sums[:count], weight_sq[5]]))
    step_norm = jnp.sqrt(jnp.concatenate([sums[count : 2 * count], step_sq[5]]))
    ratios = weight_norm / step_norm
    starts = (0, 3, 4, 6, 7, 9)
    outputs = [layer_out, tokens_grad]
    for number in range(6):
        weight = weight_list[number]
        sub_count = sub_list[number]
        ratio_part = ratios[starts[number] : starts[number] + sub_count]
        shape = (sub_count,) + (1,) * (weight.ndim - 1) if sub_count > 1 else (1,) * weight.ndim
        new_weight = weight - learn_rate * ratio_part.reshape(shape) * results[number][2]
        outputs = outputs + [
            results[number][0],
            results[number][1],
            new_weight,
            new_weight.astype(bf16),
        ]
    outputs = outputs + [jnp.stack([weight_norm, step_norm])]
    return tuple(outputs)


def solution(mesh):
    return jax.shard_map(
        shards,
        mesh=mesh,
        in_specs=(
            P(("dp", "mp"), None),
            P(("dp", "mp"), None),
            P("dp", None),
            P(None, "dp", None),
            P(None, "dp"),
            P(None, "dp", "mp"),
            P("mp", "dp"),
            P(None, "dp"),
            P(),
            P(None, "dp", None),
            P(None, "dp"),
            P(None, "dp", "mp"),
            P("mp", "dp"),
            P(None, "dp"),
            P(),
            P(None, "dp", None),
            P(None, "dp"),
            P(None, "dp", "mp"),
            P("mp", "dp"),
            P(None, "dp"),
            P(),
        ),
        out_specs=(
            P(("dp", "mp"), None),
            P(("dp", "mp"), None),
            P(None, "dp", None),
            P(None, "dp", None),
            P(None, "dp", None),
            P(None, "dp", None),
            P(None, "dp"),
            P(None, "dp"),
            P(None, "dp"),
            P(None, "dp"),
            P(None, "dp", "mp"),
            P(None, "dp", "mp"),
            P(None, "dp", "mp"),
            P(None, "dp", "mp"),
            P("mp", "dp"),
            P("mp", "dp"),
            P("mp", "dp"),
            P("mp", "dp"),
            P(None, "dp"),
            P(None, "dp"),
            P(None, "dp"),
            P(None, "dp"),
            P(),
            P(),
            P(),
            P(),
            P(),
        ),
        check_vma=False,
    )
```

time: 1080 us -> 421 us (0.39)
  waiting for transfers between devices: 697 us -> 110 us
  blocking collectives: 119 us -> 0 us
  Pallas kernels: 0 us -> 70.6 us
  matrix products: 89.8 us -> 35.3 us
  starting transfers between devices: 12.3 us -> 66.2 us
  local copies, waits for them, and re-layouts: 66.1 us -> 52.8 us
  between operations: 19.6 us -> 6.64 us
    reduce_scatter x4 -> x0, waiting for transfers between devices: 367 us -> none  [the longest x1 180 us: shards(): lax.psum_scatter(grad_expand_in, 'dp', scatter_dimension=1, tiled=True)]
    all_gather x6 -> x0, waiting for transfers between devices: 203 us -> none  [the longest x1 79.3 us: shards(): lax.all_gather(expand_in.astype(jnp.bfloat16), 'dp', axis=1, tiled=True)]
    ppermute x0 -> x74, waiting for transfers between devices: none -> 110 us  [the longest x26 43.2 us: swap(): lax.ppermute(part, 'mp', [(index, index ^ bit) for index in range(size)])]
    unnamed x19 -> x0, waiting for transfers between devices: 96.1 us -> none
    psum x2 -> x0, blocking collectives: 81.2 us -> none  [shards(): lax.psum((jnp.stack([gain_one_grad, gain_two_grad]), grad_table), ('dp',...]
    pallas_call x0 -> x9, Pallas kernels: none -> 70.6 us  [the longest x3 28.4 us: run(): pl.pallas_call(body, out_shape=[jax.ShapeDtypeStruct(shape, kind) for sha...]
    ppermute x0 -> x74, starting transfers between devices: none -> 66.2 us  [the longest x9 14.5 us: gather_dp(): ahead = lax.ppermute(ahead, 'dp', forward)]
    all_gather x3 -> x0, blocking collectives: 37.7 us -> none  [the longest x1 22.3 us: shards(): lax.all_gather(norm_gains.astype(jnp.bfloat16), 'dp', axis=1, tiled=True)]
  transfers between devices with their start and end apart: 15 -> 74, of which waited for: 15 -> 23; matrix products, arithmetic and copies ran while one was open for 15% -> 26% of each run, Pallas kernels for 0% -> 15%
where the time goes in v1:
time: 421 us; the launch traced here: 415 us
  waiting for transfers between devices  110 us (26%)
  other arithmetic  72.7 us (17%)
  Pallas kernels  70.6 us (17%)
  starting transfers between devices  66.2 us (16%)
  local copies, waits for them, and re-layouts  52.8 us (13%)
  matrix products  35.3 us (8%)
  between operations  6.64 us (2%)
    ppermute x26, waiting for transfers between devices, swap(): lax.ppermute(part, 'mp', [(index, index ^ bit) for index in range(size)])  43.2 us
    ppermute x9, waiting for transfers between devices, gather_dp(): behind = lax.ppermute(behind, 'dp', backward)  29.5 us
    pallas_call x3, Pallas kernels, run(): pl.pallas_call(body, out_shape=[jax.ShapeDtypeStruct(shape, kind) for sha...  28.4 us
    pallas_call x2, Pallas kernels, total_all(): pl.pallas_call(partial(total_kernel, (plane, line)), out_shape=jax.ShapeD...  22.7 us
    reduce_sum x6, other arithmetic, sub_squares(): return jnp.sum(flat_values * flat_values, axis=1)  15.2 us
    ppermute x9, starting transfers between devices, gather_dp(): ahead = lax.ppermute(ahead, 'dp', forward)  14.5 us
    ppermute x26, starting transfers between devices, swap(): lax.ppermute(part, 'mp', [(index, index ^ bit) for index in range(size)])  14.4 us
    dot_general x3, matrix products, matmul(): return jnp.dot(left_side, right_side, preferred_element_type=f32)  13.1 us
  transfers between devices with their start and end apart: 74, of which 23 were waited for; matrix products, arithmetic and copies ran while one was open for 26% of the time, Pallas kernels for 15%

profile of v1, /device:TPU:0, one launch (start us, length us, event | category | flops | bytes accessed | tf_op | source)
XLA Modules:
  0.0 414.7 jit_solution(9555782697332008279)
XLA Ops:
  6.2 3.6 collective-permute-done.6.refs_6_
  20.4 12.9 %collective-permute-done.5.refs_3_ = bf16[1,184,384]{2,1,0:T(8,128)(2,1)S(1)} collective-permute-done((bf16[1,184,384]{2,1,0:T(8,128)(2,1)S(1)}, bf16[1,184,384]{2,1,0:T(8,128)(2,1)S(1)}, u32[]{:S(2)}, u32[]{:S(2)}) %collective-permute-start.5) | collective-permute-done | bytes 141344 | tf_op jit(solution)/shard_map/ppermute | solution.py:123
  34.4 8.9 %gather_gains.1 = f32[8,8,256]{2,1,0:T(8,128)} custom-call(f32[8,256]{1,0:T(8,128)} %pad_convert_fusion.part_ref), custom_call_target="tpu_custom_call" | custom-call | tf_op jit(solution)/shard_map/gather_gains/pallas_call | solution.py:513
  59.6 6.5 %collective-permute-done.29.refs_5_ = bf16[1,184,896]{2,1,0:T(8,128)(2,1)} collective-permute-done((bf16[1,184,896]{2,1,0:T(8,128)(2,1)S(1)}, bf16[1,184,896]{2,1,0:T(8,128)(2,1)}, u32[]{:S(2)}, u32[]{:S(2)}) %collective-permute-start.29) | collective-permute-done | bytes 329760 | tf_op jit(solution)/shard_map/ppermute | solution.py:122
  69.2 15.2 %collective-permute-done.27.refs_3_ = bf16[1,184,896]{2,1,0:T(8,128)(2,1)S(1)} collective-permute-done((bf16[1,184,896]{2,1,0:T(8,128)(2,1)S(1)}, bf16[1,184,896]{2,1,0:T(8,128)(2,1)S(1)}, u32[]{:S(2)}, u32[]{:S(2)}) %collective-permute-start.27) | collective-permute-done | bytes 329760 | tf_op jit(solution)/shard_map/ppermute | solution.py:123
  93.0 7.1 %collective-permute-done.31.refs_7_ = bf16[1,184,512]{2,1,0:T(8,128)(2,1)S(1)} collective-permute-done((bf16[1,184,512]{2,1,0:T(8,128)(2,1)S(1)}, bf16[1,184,512]{2,1,0:T(8,128)(2,1)S(1)}, u32[]{:S(2)}, u32[]{:S(2)}) %collective-permute-start.31) | collective-permute-done | bytes 188448 | tf_op jit(solution)/shard_map/ppermute | solution.py:126
  107.5 9.2 %collective-permute-done.across_ref = bf16[192,1472]{1,0:T(8,128)(2,1)} collective-permute-done((bf16[192,1472]{1,0:T(8,128)(2,1)}, bf16[192,1472]{1,0:T(8,128)(2,1)}, u32[]{:S(2)}, u32[]{:S(2)}) %collective-permute-start) | collective-permute-done | bytes 565280 | tf_op jit(solution)/shard_map/ppermute | solution.py:176
  116.7 8.2 %collective-permute-done.35 = bf16[192,1472]{1,0:T(8,128)(2,1)} collective-permute-done((bf16[192,1472]{1,0:T(8,128)(2,1)S(1)}, bf16[192,1472]{1,0:T(8,128)(2,1)}, u32[]{:S(2)}, u32[]{:S(2)}) %collective-permute-start.35) | collective-permute-done | bytes 565280 | tf_op jit(solution)/shard_map/ppermute | solution.py:176
  134.0 11.0 %attention_forward.1 = (bf16[192,384]{1,0:T(8,128)(2,1)}, bf16[192,384]{1,0:T(8,128)(2,1)}, bf16[768,384]{1,0:T(8,128)(2,1)}, bf16[768,384]{1,0:T(8,128)(2,1)}, ...) custom-call(s32[1,2]{1,0:T(1,128)} %lens_ref.3, bf16[192,1472]{1,0:T(8,128)(2,1)} %fusion.26.own_ref, ...), custom_call_target="tpu_custom_call" | custom-call | flops 2623537152 | bytes 9043968 | tf_op jit(solution)/shard_map/attention_forward/pallas_call | solution.py:402
  145.5 5.6 %fusion.53 = f32[768,896]{1,0:T(8,128)} fusion(bf16[1472,896]{1,0:T(8,128)(2,1)S(1)} %bitcast.164, bf16[192,1472]{1,0:T(8,128)(2,1)} %collective-permute-done.37, bf16[192,1472]{1,0:T(8,128)(2,1)} %collective-permute-done.36, bf16[192,1472]{1,0:T(8,128)(2,1)} %collective-permute-done.35, bf16[192,1472]{1,0:T(8,128)(2,1)S(1)} %broadcast_select_fusion.upstream_ref), kind=kOutput, calls=%fused_computation.134 | convolution fusion | flops 2034892800 | bytes 7651328 | tf_op jit(solution)/shard_map/dot_general | solution.py:64
  152.6 4.9 %assemble.4 = bf16[2,8,184,896]{3,2,1,0:T(8,128)(2,1)} custom-call(bf16[2,184,896]{2,1,0:T(8,128)(2,1)} %copy-done.13, bf16[2,184,896]{2,1,0:T(8,128)(2,1)} %collective-permute-done.17.refs_1_, bf16[2,184,896]{2,1,0:T(8,128)(2,1)} %collective-permute-done.18.refs_2_, bf16[2,184,896]{2,1,0:T(8,128)(2,1)} %copy-done.24, bf16[2,184,896]{2,1,0:T(8,128)(2,1)} %copy-done.22, ...), custom_call_target="tpu_custom_call" | custom-call | bytes 10551296 | tf_op jit(solution)/shard_map/assemble/pallas_call | solution.py:130
  165.4 4.9 %fusion.8 = (bf16[768,896]{1,0:T(8,128)(2,1)S(1)}, bf16[768,896]{1,0:T(8,128)(2,1)S(1)}, bf16[768,896]{1,0:T(8,128)(2,1)S(1)}) fusion(f32[768,896]{1,0:T(8,128)S(1)} %copy-done.76, f32[768,896]{1,0:T(8,128)S(1)} %fusion.102, bf16[768,1472]{1,0:T(8,128)(2,1)S(1)} %constant_dynamic-update-slice_fusion, bf16[1472,896]{1,0:T(8,128)(2,1)S(1)} %bitcast.160), kind=kOutput, calls=%fused_computation.34 | convolution fusion | flops 2043740160 | bytes 14532608 | tf_op jit(solution)/shard_map/dot_general | solution.py:64
  182.1 4.1 convolution_convert_fusion.3
  186.2 4.0 convolution_convert_fusion
  235.9 8.1 %collective-permute-done.39.across_ref = bf16[192,1472]{1,0:T(8,128)(2,1)S(1)} collective-permute-done((bf16[192,1472]{1,0:T(8,128)(2,1)S(1)}, bf16[192,1472]{1,0:T(8,128)(2,1)S(1)}, u32[]{:S(2)}, u32[]{:S(2)}) %collective-permute-start.39) | collective-permute-done | bytes 565280 | tf_op jit(solution)/shard_map/ppermute | solution.py:176
  246.6 11.4 %attention_backward.1 = (f32[192,1472]{1,0:T(8,128)}, bf16[192,1472]{1,0:T(8,128)(2,1)}, bf16[192,384]{1,0:T(8,128)(2,1)}, f32[384,768]{1,0:T(8,128)}, bf16[384,...) custom-call(s32[1,2]{1,0:T(1,128)} %lens_ref.3, f32[192,1472]{1,0:T(8,128)} %slice.326.part_ref, ...), custom_call_target="tpu_custom_call" | custom-call | flops 1349517312 | bytes 10223616 | tf_op jit(solution)/shard_map/attention_backward/pallas_call | solution.py:402
  280.9 6.0 %input_backward.1 = (f32[192,1472]{1,0:T(8,128)}, bf16[192,768]{1,0:T(8,128)(2,1)}, f32[1,1472]{1,0:T(1,128)}) custom-call(f32[384,768]{1,0:T(8,128)} %get-tuple-element.50.own_ref, bf16[384,768]{1,0:T(8,128)(2,1)} %collective-permute-done.40.beside_ref, bf16[192,768]{1,0:T(8,128)(2,1)} %copy-done.47, bf16[192,384]{1,0:T(8,128)(2,1)} %get-tuple-element.52.query_grad_ref, ...), custom_call_target="tpu_custom_call" | custom-call | flops 651165696 | bytes 8478720 | tf_op jit(solution)/shard_map/input_backward/pallas_call | solution.py:402
  292.2 3.5 multiply_reduce_fusion.4
  296.6 9.5 %collective-permute-done.34 = bf16[192,1472]{1,0:T(8,128)(2,1)S(1)} collective-permute-done((bf16[192,1472]{1,0:T(8,128)(2,1)S(1)}, bf16[192,1472]{1,0:T(8,128)(2,1)S(1)}, u32[]{:S(2)}, u32[]{:S(2)}) %collective-permute-start.34) | collective-permute-done | bytes 565280 | tf_op jit(solution)/shard_map/ppermute | solution.py:176
  328.6 9.9 %collective-permute-done.51 = bf16[1,184,128]{2,1,0:T(8,128)(2,1)S(1)} collective-permute-done((bf16[1,184,128]{2,1,0:T(8,128)(2,1)S(1)}, bf16[1,184,128]{2,1,0:T(8,128)(2,1)S(1)}, u32[]{:S(2)}, u32[]{:S(2)}) %collective-permute-start.51) | collective-permute-done | bytes 47136 | tf_op jit(solution)/shard_map/ppermute | solution.py:159
  341.8 4.8 %multiply_reduce_fusion = (f32[2]{0:T(128)S(1)}, f32[2]{0:T(128)S(1)}, f32[2,184,896]{2,1,0:T(8,128)}, f32[2,184,896]{2,1,0:T(8,128)}) fusion(f32[2,184,896]{2,1,0:T(8,128)S(1)} %copy-done.3, bf16[2,184,896]{2,1,0:T(8,128)(2,1)S(1)} %collective-permute-done.65, bf16[2,184,896]{2,1,0:T(8,128)(2,1)S(1)} %collective-permute-done.61, s32[]{:T(128)S(6)} %select_n.102, ...), kind=kLoop, calls=%fused_computation.62 | loop fusion | flops 10221564 | bytes 13189140 | tf_op jit(solution)/shard_map/reduce_sum | solution.py:544
  349.3 12.4 %total.2 = f32[32,128]{1,0:T(8,128)} custom-call(f32[32,128]{1,0:T(8,128)} %fusion.66.part_ref), custom_call_target="tpu_custom_call" | custom-call | tf_op jit(solution)/shard_map/total/pallas_call | solution.py:462
  387.7 10.2 %total.3 = f32[8,128]{1,0:T(8,128)} custom-call(f32[8,128]{1,0:T(8,128)} %pad_bitcast_fusion.part_ref), custom_call_target="tpu_custom_call" | custom-call | tf_op jit(solution)/shard_map/total/pallas_call | solution.py:462
  408.5 3.5 fusion.86
  (423 shorter events, 222.8 us)
Async XLA Ops:
  12.0 45.5 %collective-permute-start.20 = (bf16[2,184,896]{2,1,0:T(8,128)(2,1)S(1)}, bf16[2,184,896]{2,1,0:T(8,128)(2,1)}, u32[]{:S(2)}, u32[]{:S(2)}) collective-permute-start(bf16[2,184,896]{2,1,0:T(8,128)(2,1)S(1)} %convert_element_type.426.refs_0_), channel_id=1, source_target_pairs={{0,8},{8,16},{16,24},{24,28},{28,20},{20,12},{12,4},{4,0},{1,9},{9... | collective-permute-start | bytes 1978376 | tf_op jit(solution)/shard_map/ppermute | solution.py:122
  13.9 44.6 %collective-permute-start.17 = (bf16[2,184,896]{2,1,0:T(8,128)(2,1)S(1)}, bf16[2,184,896]{2,1,0:T(8,128)(2,1)}, u32[]{:S(2)}, u32[]{:S(2)}) collective-permute-start(bf16[2,184,896]{2,1,0:T(8,128)(2,1)S(1)} %convert_element_type.426.refs_0_), channel_id=1, source_target_pairs={{8,0},{16,8},{24,16},{28,24},{20,28},{12,20},{4,12},{0,4},{9,1},{1... | collective-permute-start | bytes 1978376 | tf_op jit(solution)/shard_map/ppermute | solution.py:123
  16.4 26.9 %collective-permute-start.8 = (bf16[1,184,384]{2,1,0:T(8,128)(2,1)S(1)}, bf16[1,184,384]{2,1,0:T(8,128)(2,1)S(1)}, u32[]{:S(2)}, u32[]{:S(2)}) collective-permute-start(bf16[1,184,384]{2,1,0:T(8,128)(2,1)S(1)} %collective-permute-done.7.refs_5_), channel_id=1, source_target_pairs={{0,8},{8,16},{16,24},{24,28},{28,20},{20,12},{12,4},{4,0},{1,9},{9... | collective-permute-start | bytes 423944 | tf_op jit(solution)/shard_map/ppermute | solution.py:122
  18.5 36.7 %collective-permute-start.28 = (bf16[1,184,896]{2,1,0:T(8,128)(2,1)S(1)}, bf16[1,184,896]{2,1,0:T(8,128)(2,1)S(1)}, u32[]{:S(2)}, u32[]{:S(2)}) collective-permute-start(bf16[1,184,896]{2,1,0:T(8,128)(2,1)S(1)} %convert_bitcast_fusion.refs_0_), channel_id=1, source_target_pairs={{0,8},{8,16},{16,24},{24,28},{28,20},{20,12},{12,4},{4,0},{1,9},{9... | collective-permute-start | bytes 989192 | tf_op jit(solution)/shard_map/ppermute | solution.py:122
  53.0 36.2 %collective-permute-start.12 = (bf16[1,1472,384]{2,1,0:T(8,128)(2,1)}, bf16[1,1472,384]{2,1,0:T(8,128)(2,1)}, u32[]{:S(2)}, u32[]{:S(2)}) collective-permute-start(bf16[1,1472,384]{2,1,0:T(8,128)(2,1)} %bitcast.157), channel_id=1, source_target_pairs={{0,2},{1,3},{2,0},{3,1},{4,6},{5,7},{6,4},{7,5},{8,10},{9,11},{10,... | collective-permute-start | bytes 3391496 | tf_op jit(solution)/shard_map/ppermute | solution.py:176
  57.5 27.7 %collective-permute-start.21 = (bf16[2,184,896]{2,1,0:T(8,128)(2,1)}, bf16[2,184,896]{2,1,0:T(8,128)(2,1)}, u32[]{:S(2)}, u32[]{:S(2)}) collective-permute-start(bf16[2,184,896]{2,1,0:T(8,128)(2,1)} %collective-permute-done.20.refs_6_), channel_id=1, source_target_pairs={{0,8},{8,16},{16,24},{24,28},{28,20},{20,12},{12,4},{4,0},{1,9},{9... | collective-permute-start | bytes 1978376 | tf_op jit(solution)/shard_map/ppermute | solution.py:122
  58.5 32.3 %collective-permute-start.18 = (bf16[2,184,896]{2,1,0:T(8,128)(2,1)}, bf16[2,184,896]{2,1,0:T(8,128)(2,1)}, u32[]{:S(2)}, u32[]{:S(2)}) collective-permute-start(bf16[2,184,896]{2,1,0:T(8,128)(2,1)} %collective-permute-done.17.refs_1_), channel_id=1, source_target_pairs={{8,0},{16,8},{24,16},{28,24},{20,28},{12,20},{4,12},{0,4},{9,1},{1... | collective-permute-start | bytes 1978376 | tf_op jit(solution)/shard_map/ppermute | solution.py:123
  66.0 23.1 %collective-permute-start.30 = (bf16[1,184,896]{2,1,0:T(8,128)(2,1)}, bf16[1,184,896]{2,1,0:T(8,128)(2,1)S(1)}, u32[]{:S(2)}, u32[]{:S(2)}) collective-permute-start(bf16[1,184,896]{2,1,0:T(8,128)(2,1)} %collective-permute-done.29.refs_5_), channel_id=1, source_target_pairs={{0,8},{8,16},{16,24},{24,28},{28,20},{20,12},{12,4},{4,0},{1,9},{9... | collective-permute-start | bytes 989192 | tf_op jit(solution)/shard_map/ppermute | solution.py:122
  89.1 35.8 %collective-permute-start.11 = (bf16[1,1472,384]{2,1,0:T(8,128)(2,1)}, bf16[1,1472,384]{2,1,0:T(8,128)(2,1)}, u32[]{:S(2)}, u32[]{:S(2)}) collective-permute-start(bf16[1,1472,384]{2,1,0:T(8,128)(2,1)} %bitcast.158), channel_id=1, source_target_pairs={{0,1},{1,0},{2,3},{3,2},{4,5},{5,4},{6,7},{7,6},{8,9},{9,8},{10,11... | collective-permute-start | bytes 3391496 | tf_op jit(solution)/shard_map/ppermute | solution.py:176
  89.2 36.2 %collective-permute-start.13 = (bf16[1,1472,384]{2,1,0:T(8,128)(2,1)}, bf16[1,1472,384]{2,1,0:T(8,128)(2,1)}, u32[]{:S(2)}, u32[]{:S(2)}) collective-permute-start(bf16[1,1472,384]{2,1,0:T(8,128)(2,1)} %collective-permute-done.12), channel_id=1, source_target_pairs={{0,1},{1,0},{2,3},{3,2},{4,5},{5,4},{6,7},{7,6},{8,9},{9,8},{10,11... | collective-permute-start | bytes 3391496 | tf_op jit(solution)/shard_map/ppermute | solution.py:176
  100.6 24.3 %collective-permute-start.35 = (bf16[192,1472]{1,0:T(8,128)(2,1)S(1)}, bf16[192,1472]{1,0:T(8,128)(2,1)}, u32[]{:S(2)}, u32[]{:S(2)}) collective-permute-start(bf16[192,1472]{1,0:T(8,128)(2,1)S(1)} %broadcast_select_fusion.upstream_ref), channel_id=1, source_target_pairs={{0,2},{1,3},{2,0},{3,1},{4,6},{5,7},{6,4},{7,5},{8,10},{9,11},{10,... | collective-permute-start | bytes 1695752 | tf_op jit(solution)/shard_map/ppermute | solution.py:176
  107.5 24.1 %collective-permute-start.1 = (bf16[192,1472]{1,0:T(8,128)(2,1)S(1)}, bf16[192,1472]{1,0:T(8,128)(2,1)S(1)}, u32[]{:S(2)}, u32[]{:S(2)}) collective-permute-start(bf16[192,1472]{1,0:T(8,128)(2,1)S(1)} %copy-done.38), channel_id=1, source_target_pairs={{0,1},{1,0},{2,3},{3,2},{4,5},{5,4},{6,7},{7,6},{8,9},{9,8},{10,11... | collective-permute-start | bytes 1695752 | tf_op jit(solution)/shard_map/ppermute | solution.py:176
  116.7 28.8 %collective-permute-start.36 = (bf16[192,1472]{1,0:T(8,128)(2,1)S(1)}, bf16[192,1472]{1,0:T(8,128)(2,1)}, u32[]{:S(2)}, u32[]{:S(2)}) collective-permute-start(bf16[192,1472]{1,0:T(8,128)(2,1)S(1)} %broadcast_select_fusion.upstream_ref), channel_id=1, source_target_pairs={{0,1},{1,0},{2,3},{3,2},{4,5},{5,4},{6,7},{7,6},{8,9},{9,8},{10,11... | collective-permute-start | bytes 1695752 | tf_op jit(solution)/shard_map/ppermute | solution.py:176
  125.4 25.7 %collective-permute-start.23 = (bf16[2,184,512]{2,1,0:T(8,128)(2,1)S(1)}, bf16[2,184,512]{2,1,0:T(8,128)(2,1)S(1)}, u32[]{:S(2)}, u32[]{:S(2)}) collective-permute-start(bf16[2,184,512]{2,1,0:T(8,128)(2,1)S(1)} %slice.314), channel_id=1, source_target_pairs={{0,8},{8,16},{16,24},{24,28},{28,20},{20,12},{12,4},{4,0},{1,9},{9... | collective-permute-start | bytes 1130504 | tf_op jit(solution)/shard_map/ppermute | solution.py:126
  181.7 41.8 %collective-permute-start.38 = (bf16[384,1472]{0,1:T(8,128)(2,1)}, bf16[384,1472]{0,1:T(8,128)(2,1)}, u32[]{:S(2)}, u32[]{:S(2)}) collective-permute-start(bf16[384,1472]{0,1:T(8,128)(2,1)} %slice.396), channel_id=1, source_target_pairs={{0,1},{1,0},{2,3},{3,2},{4,5},{5,4},{6,7},{7,6},{8,9},{9,8},{10,11... | collective-permute-start | bytes 3391496 | tf_op jit(solution)/shard_map/ppermute | solution.py:176
  192.0 22.9 %collective-permute-start.70 = (bf16[1,184,384]{2,1,0:T(8,128)(2,1)}, bf16[1,184,384]{2,1,0:T(8,128)(2,1)}, u32[]{:S(2)}, u32[]{:S(2)}) collective-permute-start(bf16[1,184,384]{2,1,0:T(8,128)(2,1)} %slice.350), channel_id=1, source_target_pairs={{8,0},{16,8},{24,16},{28,24},{20,28},{12,20},{4,12},{0,4},{9,1},{1... | collective-permute-start | bytes 423944 | tf_op jit(solution)/shard_map/ppermute | solution.py:159
  207.2 21.9 %collective-permute-start.58 = (bf16[2,184,512]{2,1,0:T(8,128)(2,1)}, bf16[2,184,512]{2,1,0:T(8,128)(2,1)}, u32[]{:S(2)}, u32[]{:S(2)}) collective-permute-start(bf16[2,184,512]{2,1,0:T(8,128)(2,1)} %slice.340), channel_id=1, source_target_pairs={{0,8},{8,16},{16,24},{24,28},{28,20},{20,12},{12,4},{4,0},{1,9},{9... | collective-permute-start | bytes 1130504 | tf_op jit(solution)/shard_map/ppermute | solution.py:158
  214.9 51.4 %collective-permute-start.33 = (bf16[384,1472]{0,1:T(8,128)(2,1)}, bf16[384,1472]{0,1:T(8,128)(2,1)}, u32[]{:S(2)}, u32[]{:S(2)}) collective-permute-start(bf16[384,1472]{0,1:T(8,128)(2,1)} %copy.80), channel_id=1, source_target_pairs={{0,1},{1,0},{2,3},{3,2},{4,5},{5,4},{6,7},{7,6},{8,9},{9,8},{10,11... | collective-permute-start | bytes 3391496 | tf_op jit(solution)/shard_map/ppermute | solution.py:176
  216.8 41.3 %collective-permute-start.71 = (bf16[1,184,896]{2,1,0:T(8,128)(2,1)}, bf16[1,184,896]{2,1,0:T(8,128)(2,1)}, u32[]{:S(2)}, u32[]{:S(2)}) collective-permute-start(bf16[1,184,896]{2,1,0:T(8,128)(2,1)} %pad_maximum_fusion.11), channel_id=1, source_target_pairs={{8,0},{16,8},{24,16},{28,24},{20,28},{12,20},{4,12},{0,4},{9,1},{1... | collective-permute-start | bytes 989192 | tf_op jit(solution)/shard_map/ppermute | solution.py:170
  223.5 37.7 %collective-permute-start.63 = (bf16[2,184,896]{2,1,0:T(8,128)(2,1)}, bf16[2,184,896]{2,1,0:T(8,128)(2,1)}, u32[]{:S(2)}, u32[]{:S(2)}) collective-permute-start(bf16[2,184,896]{2,1,0:T(8,128)(2,1)} %pad_maximum_fusion.4), channel_id=1, source_target_pairs={{8,0},{16,8},{24,16},{28,24},{20,28},{12,20},{4,12},{0,4},{9,1},{1... | collective-permute-start | bytes 1978376 | tf_op jit(solution)/shard_map/ppermute | solution.py:170
  232.7 29.9 %collective-permute-start.59 = (bf16[2,184,896]{2,1,0:T(8,128)(2,1)}, bf16[2,184,896]{2,1,0:T(8,128)(2,1)}, u32[]{:S(2)}, u32[]{:S(2)}) collective-permute-start(bf16[2,184,896]{2,1,0:T(8,128)(2,1)} %pad_maximum_fusion.3), channel_id=1, source_target_pairs={{0,8},{8,16},{16,24},{24,28},{28,20},{20,12},{12,4},{4,0},{1,9},{9... | collective-permute-start | bytes 1978376 | tf_op jit(solution)/shard_map/ppermute | solution.py:169
  261.3 27.1 %collective-permute-start.69 = (bf16[1,184,896]{2,1,0:T(8,128)(2,1)}, bf16[1,184,896]{2,1,0:T(8,128)(2,1)}, u32[]{:S(2)}, u32[]{:S(2)}) collective-permute-start(bf16[1,184,896]{2,1,0:T(8,128)(2,1)} %get-tuple-element.167), channel_id=1, source_target_pairs={{0,8},{8,16},{16,24},{24,28},{28,20},{20,12},{12,4},{4,0},{1,9},{9... | collective-permute-start | bytes 989192 | tf_op jit(solution)/shard_map/ppermute | solution.py:169
  265.4 43.2 %collective-permute-start.60 = (bf16[2,184,896]{2,1,0:T(8,128)(2,1)}, bf16[2,184,896]{2,1,0:T(8,128)(2,1)}, u32[]{:S(2)}, u32[]{:S(2)}) collective-permute-start(bf16[2,184,896]{2,1,0:T(8,128)(2,1)} %get-tuple-element.156), channel_id=1, source_target_pairs={{0,8},{8,16},{16,24},{24,28},{28,20},{20,12},{12,4},{4,0},{1,9},{9... | collective-permute-start | bytes 1978376 | tf_op jit(solution)/shard_map/ppermute | solution.py:169
  266.3 42.3 %collective-permute-start.64 = (bf16[2,184,896]{2,1,0:T(8,128)(2,1)}, bf16[2,184,896]{2,1,0:T(8,128)(2,1)}, u32[]{:S(2)}, u32[]{:S(2)}) collective-permute-start(bf16[2,184,896]{2,1,0:T(8,128)(2,1)} %get-tuple-element.157), channel_id=1, source_target_pairs={{8,0},{16,8},{24,16},{28,24},{20,28},{12,20},{4,12},{0,4},{9,1},{1... | collective-permute-start | bytes 1978376 | tf_op jit(solution)/shard_map/ppermute | solution.py:170
  (127 other events, 1819.8 us)
